TPU v7x, 128 devices: a whole 4x4x4 slice. The times are simulated.
128 devices in a mesh: feat: 16 (over z, y), batch: 8 (over x, core).
Axes of the slice: x: 4, y: 4, z: 4, core: 2. Of those that a mesh axis runs over, the one named last changes fastest.
Arguments:
- features: bfloat16 [768, 131072], P('feat', 'batch'), may hold values from -6 to 6
- sampled_slots: int32 [8, 8, 16, 4096], P(None, 'batch'), may hold values from 0 to 2047
- block_index: int32 [8, 8, 32, 16], P(None, 'batch'), may hold values from 0 to 127
- counts: int32 [8, 8, 4096], replicated, may hold values from 1 to 16
- weight: bfloat16 [768, 1024], P('feat'), may hold values from -1.75 to 1.75
- cotangent: bfloat16 [32768, 1024], P(('feat', 'batch')), may hold values from -0.59765625 to 0.59765625
Outputs:
- hidden: bfloat16 [32768, 1024], P(('feat', 'batch'))
- weight_grad: float32 [768, 1024], P('feat')
Inputs may be any that keep to these rules, and one draw needn't show every extreme that they name: A stored value v = sampled_slots[g, p, s, j] names entry v // 128 of block_index's list for block j // 128, and node v % 128 of that tile.
All inputs are finite; a program needn't handle non-finite values.
Results may differ from a plain program's by a relative error of at most 0.0053.
Values may be sent and summed in bfloat16 or wider, within the bound.
A program may use at most 128 MiB of HBM per device.

v0:
```python
from functools import partial
import math

import jax
import jax.numpy as jnp
from jax import lax
from jax.sharding import PartitionSpec as P


def rowblock_sum(blocks, tile_ids, chosen, row_counts):
    feat_width = blocks.shape[0]
    tile_span = tile_ids.shape[0] * 128
    gathered = jnp.take(blocks, tile_ids, axis=1).reshape(feat_width, tile_span)
    live_mask = lax.broadcasted_iota(jnp.int32, chosen.shape, 0) < row_counts[None, :]
    columns = lax.broadcasted_iota(jnp.int32, (1, tile_span, 1), 1)
    matches = (chosen[:, None, :] == columns) & live_mask[:, None, :]
    adjacency = jnp.sum(matches.astype(jnp.int32), axis=0).astype(jnp.bfloat16)
    return jnp.dot(gathered, adjacency, preferred_element_type=jnp.float32)


def per_device(features, sampled_slots, block_index, counts, weight, cotangent):
    part_index = lax.axis_index("batch")
    feat_width, node_count = features.shape
    blocks = features.reshape(feat_width, node_count // 128, 128)
    slot_total = sampled_slots.shape[2]
    group_rows = sampled_slots.shape[3]
    row_blocks = group_rows // 128
    tile_count = block_index.shape[3]
    local_counts = lax.dynamic_index_in_dim(counts, part_index, 1, keepdims=False)
    amount = 1 * lax.axis_size("batch")
    chosen = sampled_slots[:, 0]
    chosen = chosen.reshape(amount, slot_total, row_blocks, 128)
    chosen = jnp.transpose(chosen, (0, 2, 1, 3)).reshape(amount * row_blocks, slot_total, 128)
    tile_ids = block_index[:, 0]
    tile_ids = tile_ids.reshape(amount * row_blocks, tile_count)
    row_counts = local_counts
    row_counts = row_counts.reshape(amount * row_blocks, 128)
    total = amount * row_blocks
    per_turn = math.gcd(total, 16)
    turns = total // per_turn

    def one_turn(packed):
        return jax.vmap(partial(rowblock_sum, blocks))(*packed)

    result = lax.map(
        one_turn,
        (
            tile_ids.reshape(turns, per_turn, tile_count),
            chosen.reshape(turns, per_turn, slot_total, 128),
            row_counts.reshape(turns, per_turn, 128),
        ),
    )
    result = result.reshape(amount, row_blocks, feat_width, 128)
    summed = lax.psum_scatter(
        jnp.transpose(result, (0, 2, 1, 3)).reshape(amount, feat_width, group_rows),
        "batch",
        scatter_dimension=0,
        tiled=True,
    )[0]
    totals = jnp.sum(counts[part_index], axis=0).astype(jnp.float32)
    aggregate = (summed / totals[None, :]).astype(jnp.bfloat16)
    picked = aggregate
    preact = lax.psum_scatter(
        jnp.einsum("dr,dh->rh", picked, weight, preferred_element_type=jnp.float32),
        "feat",
        scatter_dimension=0,
        tiled=True,
    )
    sigmoid_val = jax.nn.sigmoid(preact)
    hidden = (preact * sigmoid_val).astype(jnp.bfloat16)
    pre_grad = (
        cotangent.astype(jnp.float32) * sigmoid_val * (1.0 + preact * (1.0 - sigmoid_val))
    ).astype(jnp.bfloat16)
    picked = aggregate
    grad_part = jnp.dot(
        picked,
        lax.all_gather(pre_grad, "feat", axis=0, tiled=True),
        preferred_element_type=jnp.float32,
    )
    weight_grad = lax.psum(grad_part, "batch")
    return (hidden, weight_grad)


def solution(mesh):
    placed = (
        P("feat", "batch"),
        P(None, "batch", None, None),
        P(None, "batch", None, None),
        P(),
        P("feat", None),
        P(("feat", "batch"), None),
    )
    return jax.shard_map(
        per_device,
        mesh=mesh,
        in_specs=placed,
        out_specs=(P(("feat", "batch"), None), P("feat", None)),
        check_vma=False,
    )
```

profile of v0, /device:TPU:1, one launch (start us, length us, event | category | flops | bytes accessed | tf_op | source)
XLA Modules:
  0.0 1326.0 jit_solution(13312584885556614566)
XLA Ops:
  7.2 2.1 copy.28
  9.3 2.5 copy.22
  12.2 1.3 constant_dynamic-slice_fusion
  13.5 988.0 %while.10 = (s32[]{:T(128)}, f32[16,16,48,128]{3,2,1,0:T(8,128)}, s32[16,16,16]{2,1,0:T(8,128)S(1)}, bf16[48,128,128]{2,0,1:T(8,128)(2,1)S(1)}, s32[16,16,16,128...) while((s32[]{:T(128)}, f32[16,16,48,128]{3,2,1,0:T(8,128)}, s32[16,16,16]{2,1,0:T(8,128)S(1)}, ...), condition=%wide.region_2.3_spmd, body=%wide.region_0.2_spmd.sunk | while | flops 672697600 | bytes 44011612 | solution.py:45
  13.6 0.9 dynamic-slice_bitcast_fusion.4
  14.5 48.9 %convert_reduce_fusion.2 = s32[16,2048,128]{2,1,0:T(8,128)} fusion(s32[16,16,128]{2,1,0:T(8,128)S(1)} %dynamic-slice_bitcast_fusion.4, pred[16,16,128]{2,1,0:T(8,128)(4,1)S(1)} %iota_compare_fusion.3), kind=kLoop, calls=%fused_computation.1.clone.1 | loop fusion | flops 264241152 | bytes 16941056 | tf_op jit(solution)/shard_map/while/body/eval_jaxpr/vmap()/reduce_sum | solution.py:17
  63.6 2.7 gather_fusion
  66.4 8.9 fusion.24
  76.3 48.9 %convert_reduce_fusion.2 = s32[16,2048,128]{2,1,0:T(8,128)} fusion(s32[16,16,128]{2,1,0:T(8,128)S(1)} %dynamic-slice_bitcast_fusion.4, pred[16,16,128]{2,1,0:T(8,128)(4,1)S(1)} %iota_compare_fusion.3), kind=kLoop, calls=%fused_computation.1.clone.1 | loop fusion | flops 264241152 | bytes 16941056 | tf_op jit(solution)/shard_map/while/body/eval_jaxpr/vmap()/reduce_sum | solution.py:17
  125.3 2.7 gather_fusion
  128.1 9.0 fusion.24
  138.0 48.9 %convert_reduce_fusion.2 = s32[16,2048,128]{2,1,0:T(8,128)} fusion(s32[16,16,128]{2,1,0:T(8,128)S(1)} %dynamic-slice_bitcast_fusion.4, pred[16,16,128]{2,1,0:T(8,128)(4,1)S(1)} %iota_compare_fusion.3), kind=kLoop, calls=%fused_computation.1.clone.1 | loop fusion | flops 264241152 | bytes 16941056 | tf_op jit(solution)/shard_map/while/body/eval_jaxpr/vmap()/reduce_sum | solution.py:17
  187.1 2.7 gather_fusion
  189.9 8.9 fusion.24
  199.8 48.9 %convert_reduce_fusion.2 = s32[16,2048,128]{2,1,0:T(8,128)} fusion(s32[16,16,128]{2,1,0:T(8,128)S(1)} %dynamic-slice_bitcast_fusion.4, pred[16,16,128]{2,1,0:T(8,128)(4,1)S(1)} %iota_compare_fusion.3), kind=kLoop, calls=%fused_computation.1.clone.1 | loop fusion | flops 264241152 | bytes 16941056 | tf_op jit(solution)/shard_map/while/body/eval_jaxpr/vmap()/reduce_sum | solution.py:17
  248.8 2.7 gather_fusion
  251.6 9.0 fusion.24
  261.5 48.9 %convert_reduce_fusion.2 = s32[16,2048,128]{2,1,0:T(8,128)} fusion(s32[16,16,128]{2,1,0:T(8,128)S(1)} %dynamic-slice_bitcast_fusion.4, pred[16,16,128]{2,1,0:T(8,128)(4,1)S(1)} %iota_compare_fusion.3), kind=kLoop, calls=%fused_computation.1.clone.1 | loop fusion | flops 264241152 | bytes 16941056 | tf_op jit(solution)/shard_map/while/body/eval_jaxpr/vmap()/reduce_sum | solution.py:17
  310.6 2.7 gather_fusion
  313.4 8.9 fusion.24
  323.3 48.9 %convert_reduce_fusion.2 = s32[16,2048,128]{2,1,0:T(8,128)} fusion(s32[16,16,128]{2,1,0:T(8,128)S(1)} %dynamic-slice_bitcast_fusion.4, pred[16,16,128]{2,1,0:T(8,128)(4,1)S(1)} %iota_compare_fusion.3), kind=kLoop, calls=%fused_computation.1.clone.1 | loop fusion | flops 264241152 | bytes 16941056 | tf_op jit(solution)/shard_map/while/body/eval_jaxpr/vmap()/reduce_sum | solution.py:17
  372.3 2.7 gather_fusion
  375.1 9.0 fusion.24
  385.1 48.9 %convert_reduce_fusion.2 = s32[16,2048,128]{2,1,0:T(8,128)} fusion(s32[16,16,128]{2,1,0:T(8,128)S(1)} %dynamic-slice_bitcast_fusion.4, pred[16,16,128]{2,1,0:T(8,128)(4,1)S(1)} %iota_compare_fusion.3), kind=kLoop, calls=%fused_computation.1.clone.1 | loop fusion | flops 264241152 | bytes 16941056 | tf_op jit(solution)/shard_map/while/body/eval_jaxpr/vmap()/reduce_sum | solution.py:17
  434.1 2.7 gather_fusion
  436.9 8.9 fusion.24
  446.8 48.9 %convert_reduce_fusion.2 = s32[16,2048,128]{2,1,0:T(8,128)} fusion(s32[16,16,128]{2,1,0:T(8,128)S(1)} %dynamic-slice_bitcast_fusion.4, pred[16,16,128]{2,1,0:T(8,128)(4,1)S(1)} %iota_compare_fusion.3), kind=kLoop, calls=%fused_computation.1.clone.1 | loop fusion | flops 264241152 | bytes 16941056 | tf_op jit(solution)/shard_map/while/body/eval_jaxpr/vmap()/reduce_sum | solution.py:17
  495.8 2.7 gather_fusion
  498.6 9.0 fusion.24
  508.6 48.9 %convert_reduce_fusion.2 = s32[16,2048,128]{2,1,0:T(8,128)} fusion(s32[16,16,128]{2,1,0:T(8,128)S(1)} %dynamic-slice_bitcast_fusion.4, pred[16,16,128]{2,1,0:T(8,128)(4,1)S(1)} %iota_compare_fusion.3), kind=kLoop, calls=%fused_computation.1.clone.1 | loop fusion | flops 264241152 | bytes 16941056 | tf_op jit(solution)/shard_map/while/body/eval_jaxpr/vmap()/reduce_sum | solution.py:17
  557.6 2.7 gather_fusion
  560.4 8.9 fusion.24
  570.3 48.9 %convert_reduce_fusion.2 = s32[16,2048,128]{2,1,0:T(8,128)} fusion(s32[16,16,128]{2,1,0:T(8,128)S(1)} %dynamic-slice_bitcast_fusion.4, pred[16,16,128]{2,1,0:T(8,128)(4,1)S(1)} %iota_compare_fusion.3), kind=kLoop, calls=%fused_computation.1.clone.1 | loop fusion | flops 264241152 | bytes 16941056 | tf_op jit(solution)/shard_map/while/body/eval_jaxpr/vmap()/reduce_sum | solution.py:17
  619.3 2.7 gather_fusion
  622.1 8.9 fusion.24
  632.0 48.9 %convert_reduce_fusion.2 = s32[16,2048,128]{2,1,0:T(8,128)} fusion(s32[16,16,128]{2,1,0:T(8,128)S(1)} %dynamic-slice_bitcast_fusion.4, pred[16,16,128]{2,1,0:T(8,128)(4,1)S(1)} %iota_compare_fusion.3), kind=kLoop, calls=%fused_computation.1.clone.1 | loop fusion | flops 264241152 | bytes 16941056 | tf_op jit(solution)/shard_map/while/body/eval_jaxpr/vmap()/reduce_sum | solution.py:17
  681.1 2.7 gather_fusion
  683.9 8.9 fusion.24
  693.8 48.9 %convert_reduce_fusion.2 = s32[16,2048,128]{2,1,0:T(8,128)} fusion(s32[16,16,128]{2,1,0:T(8,128)S(1)} %dynamic-slice_bitcast_fusion.4, pred[16,16,128]{2,1,0:T(8,128)(4,1)S(1)} %iota_compare_fusion.3), kind=kLoop, calls=%fused_computation.1.clone.1 | loop fusion | flops 264241152 | bytes 16941056 | tf_op jit(solution)/shard_map/while/body/eval_jaxpr/vmap()/reduce_sum | solution.py:17
  742.8 2.7 gather_fusion
  745.6 9.0 fusion.24
  755.5 48.9 %convert_reduce_fusion.2 = s32[16,2048,128]{2,1,0:T(8,128)} fusion(s32[16,16,128]{2,1,0:T(8,128)S(1)} %dynamic-slice_bitcast_fusion.4, pred[16,16,128]{2,1,0:T(8,128)(4,1)S(1)} %iota_compare_fusion.3), kind=kLoop, calls=%fused_computation.1.clone.1 | loop fusion | flops 264241152 | bytes 16941056 | tf_op jit(solution)/shard_map/while/body/eval_jaxpr/vmap()/reduce_sum | solution.py:17
  804.6 2.7 gather_fusion
  807.4 9.0 fusion.24
  817.3 48.9 %convert_reduce_fusion.2 = s32[16,2048,128]{2,1,0:T(8,128)} fusion(s32[16,16,128]{2,1,0:T(8,128)S(1)} %dynamic-slice_bitcast_fusion.4, pred[16,16,128]{2,1,0:T(8,128)(4,1)S(1)} %iota_compare_fusion.3), kind=kLoop, calls=%fused_computation.1.clone.1 | loop fusion | flops 264241152 | bytes 16941056 | tf_op jit(solution)/shard_map/while/body/eval_jaxpr/vmap()/reduce_sum | solution.py:17
  866.3 2.7 gather_fusion
  869.1 8.9 fusion.24
  879.0 48.9 %convert_reduce_fusion.2 = s32[16,2048,128]{2,1,0:T(8,128)} fusion(s32[16,16,128]{2,1,0:T(8,128)S(1)} %dynamic-slice_bitcast_fusion.4, pred[16,16,128]{2,1,0:T(8,128)(4,1)S(1)} %iota_compare_fusion.3), kind=kLoop, calls=%fused_computation.1.clone.1 | loop fusion | flops 264241152 | bytes 16941056 | tf_op jit(solution)/shard_map/while/body/eval_jaxpr/vmap()/reduce_sum | solution.py:17
  928.1 2.7 gather_fusion
  930.9 9.0 fusion.24
  940.8 48.9 %convert_reduce_fusion.2 = s32[16,2048,128]{2,1,0:T(8,128)} fusion(s32[16,16,128]{2,1,0:T(8,128)S(1)} %dynamic-slice_bitcast_fusion.4, pred[16,16,128]{2,1,0:T(8,128)(4,1)S(1)} %iota_compare_fusion.3), kind=kLoop, calls=%fused_computation.1.clone.1 | loop fusion | flops 264241152 | bytes 16941056 | tf_op jit(solution)/shard_map/while/body/eval_jaxpr/vmap()/reduce_sum | solution.py:17
  989.8 2.7 gather_fusion
  992.6 8.9 fusion.24
  1001.6 7.3 copy.41
  1008.9 7.2 reshape.63
  1016.1 0.9 dynamic-slice_reduce_fusion
  1017.1 44.3 %reduce-scatter.3.cloned.1.call-done = f32[1,48,4096]{2,1,0:T(8,128)} async-done(((f32[8,48,4096]{2,1,0:T(8,128)}), f32[1,48,4096]{2,1,0:T(8,128)}) %reduce-scatter.3.cloned.1.call-update) | async-done | bytes 786448 | tf_op jit(solution)/shard_map/reduce_scatter | solution.py:54
  1061.3 9.2 fusion.16
  1070.6 110.8 %reduce-scatter.5.cloned.1.call-done = f32[256,1024]{1,0:T(8,128)} async-done(((f32[4096,1024]{1,0:T(8,128)}), f32[256,1024]{1,0:T(8,128)}) %reduce-scatter.5.cloned.1.call-update) | async-done | bytes 1048592 | tf_op jit(solution)/shard_map/reduce_scatter | solution.py:63
  1181.4 2.7 multiply_convert_fusion
  1184.2 70.7 %all-gather.2.cloned.1.call-done = bf16[4096,1024]{1,0:T(8,128)(2,1)} async-done(((bf16[256,1024]{1,0:T(8,128)(2,1)}), bf16[4096,1024]{1,0:T(8,128)(2,1)}) %all-gather.2.cloned.1.call-update) | async-done | bytes 8388624 | tf_op jit(solution)/shard_map/all_gather | solution.py:77
  1254.9 5.6 fusion.14
  1260.6 57.2 %all-reduce.2.cloned.1.call-done = f32[48,1024]{1,0:T(8,128)} async-done(((f32[48,1024]{1,0:T(8,128)}), f32[48,1024]{1,0:T(8,128)}) %all-reduce.2.cloned.1.call-update) | async-done | bytes 196624 | tf_op jit(solution)/shard_map/psum | solution.py:80
  1317.8 1.6 copy.56
  (167 shorter events, 18.4 us)
Async XLA Ops:
  7.2 4.7 copy-start
  7.2 4.9 copy-start.5
  7.2 1054.1 %reduce-scatter.3.cloned.1.call-start = ((), (), s32[]{:S(2)}) async-start(), calls=%async_computation.2 | async-start | bytes 7077888 | tf_op jit(solution)/shard_map/reduce_scatter | solution.py:54
  1016.0 45.3 %copy-start.4 = (bf16[48,1024]{1,0:T(8,128)(2,1)S(1)}, bf16[48,1024]{1,0:T(8,128)(2,1)}, u32[]{:S(2)}) copy-start(bf16[48,1024]{1,0:T(8,128)(2,1)} %param.12) | copy-start | bytes 294916
  1016.1 165.4 %reduce-scatter.5.cloned.1.call-start = ((), (), s32[]{:S(2)}) async-start(), calls=%async_computation.3 | async-start | bytes 17825792 | tf_op jit(solution)/shard_map/reduce_scatter | solution.py:63
  1070.5 110.9 %copy-start.3 = (bf16[256,1024]{1,0:T(8,128)(2,1)S(1)}, bf16[256,1024]{1,0:T(8,128)(2,1)}, u32[]{:S(2)}) copy-start(bf16[256,1024]{1,0:T(8,128)(2,1)} %param.13) | copy-start | bytes 1572868
  1070.6 184.4 %copy-start.2 = (f32[1,48,4096]{2,1,0:T(8,128)S(1)}, f32[1,48,4096]{2,1,0:T(8,128)}, u32[]{:S(2)}) copy-start(f32[1,48,4096]{2,1,0:T(8,128)} %reduce-scatter.3.cloned.1.call-done) | copy-start | bytes 2359300
  1070.6 184.4 %all-gather.2.cloned.1.call-start = ((), (), s32[]{:S(2)}) async-start(), calls=%async_computation.4 | async-start | bytes 8912896 | tf_op jit(solution)/shard_map/all_gather | solution.py:77
  1184.2 135.3 %copy-start.1 = (bf16[48,16384]{1,0:T(8,128)(2,1)S(1)}, bf16[48,16384]{1,0:T(8,128)(2,1)}, u32[]{:S(2)}) copy-start(bf16[48,16384]{1,0:T(8,128)(2,1)} %param.8) | copy-start | bytes 4718596
  1184.2 133.6 %all-reduce.2.cloned.1.call-start = ((), (), s32[]{:S(2)}) async-start(), calls=%async_computation.5 | async-start | bytes 393216 | tf_op jit(solution)/shard_map/psum | solution.py:80
Sparse Core Ops, SparseCore 0:
  1016.2 45.0 reduce-scatter.2
  1070.7 110.6 reduce-scatter.4
  1184.3 70.5 all-gather.1
  1260.7 57.0 all-reduce.1
where the time goes:
time: 1330 us
  other arithmetic  787 us (59%)
  waiting for transfers between devices  283 us (21%)
  matrix products  158 us (12%)
  local copies, waits for them, and re-layouts  83 us (6%)
  between operations  13.8 us (1%)
    reduce_sum x16, other arithmetic, rowblock_sum(): adjacency = jnp.sum(matches.astype(jnp.int32), axis=0).astype(jnp.bfloat16)  783 us
    dot_general x16, matrix products, rowblock_sum(): return jnp.dot(gathered, adjacency, preferred_element_type=jnp.float32)  143 us
    reduce_scatter x1, waiting for transfers between devices, per_device(): lax.psum_scatter(jnp.einsum('dr,dh->rh', picked, weight, preferred_elemen...  111 us
    all_gather x1, waiting for transfers between devices, per_device(): lax.all_gather(pre_grad, 'feat', axis=0, tiled=True)  70.7 us
    psum x1, waiting for transfers between devices, per_device(): weight_grad = lax.psum(grad_part, 'batch')  57.2 us
    reduce_scatter x1, waiting for transfers between devices, per_device(): lax.psum_scatter(jnp.transpose(result, (0, 2, 1, 3)).reshape(amount, feat...  44.3 us
    gather x16, local copies, waits for them, and re-layouts, rowblock_sum(): gathered = jnp.take(blocks, tile_ids, axis=1).reshape(feat_width, tile_span)  42.6 us
  transfers between devices with their start and end apart: 4, of which 4 were waited for; matrix products, arithmetic and copies ran while one was open for 0% of the time, Pallas kernels for 0%

commit v1 on v0

v1 whole, which is shorter than its diff:
```python
import jax
import jax.numpy as jnp
from jax import lax
from jax.experimental import pallas as pl
from jax.experimental.pallas import tpu as pltpu
from jax.sharding import PartitionSpec as P

BF = jnp.bfloat16
F32 = jnp.float32
NT = (((1,), (1,)), ((), ()))


def shift(array, axis, move):
    size = lax.axis_size(axis)
    return lax.ppermute(array, axis, [(at, move(at)) for at in range(size)])


def along_z(array, step):
    return shift(array, "feat", lambda at: (at + 4 * step) % 16)


def along_y(array, step):
    return shift(array, "feat", lambda at: at // 4 * 4 + (at + step) % 4)


def along_x(array, step):
    return shift(array, "batch", lambda at: (at + 2 * step) % 8)


def flip(array, bit):
    return shift(array, "batch", lambda at: at ^ bit)


def edge_codes(slots, used):
    slot_row = lax.broadcasted_iota(jnp.int32, slots.shape, 0) & 15
    lane = lax.broadcasted_iota(jnp.int32, slots.shape, 1)
    height = slots.shape[0]
    value = jnp.where(slot_row < used, slots, -1)
    for bit in range(4):
        rows, lanes = 1 << bit, 8 << bit
        row_bit = (slot_row >> bit) & 1
        lane_bit = (lane >> (bit + 3)) & 1
        later = pltpu.roll(pltpu.roll(value, height - rows, 0), lanes, 1)
        earlier = pltpu.roll(pltpu.roll(value, rows, 0), 128 - lanes, 1)
        value = jnp.where(row_bit < lane_bit, later, jnp.where(row_bit > lane_bit, earlier, value))
    return (value >> 7) * 8 + (lane & 7), value & 127


def onehot(code):
    rows = lax.broadcasted_iota(jnp.int32, (128, 128), 0).astype(BF)
    match = jnp.broadcast_to(code.astype(BF), (128, 128)) == rows
    return jnp.where(match, BF(1), BF(0))


def group_at(step, where):
    other = 1 - step // 4
    return lax.rem(where[0] + step % 4, 4) * 2 + lax.rem(where[1] + other, 2)


def sum_kernel(where, tiles, slots, counts, f0, f1, f2, f3, out, tile_codes, node_codes, adjacency):
    group = group_at(pl.program_id(0), where)
    part = where[0] * 2 + where[1]
    used = counts[0, pl.ds(part, 1), :]
    tile_code, node_code = edge_codes(
        jnp.concatenate([slots[0, 0, :, b * 128:b * 128 + 128] for b in range(8)], 0),
        jnp.concatenate([jnp.broadcast_to(used[:, b * 128:b * 128 + 128], (16, 128)) for b in range(8)], 0),
    )
    tile_codes[...] = tile_code
    node_codes[...] = node_code

    def build(block, slot):
        blank = jnp.zeros((128, 128), BF)
        for pair in range(8):
            row = block * 16 + 2 * pair
            tile_a, tile_b = onehot(tile_codes[pl.ds(row, 1)]), onehot(tile_codes[pl.ds(row + 1, 1)])
            node_a, node_b = onehot(node_codes[pl.ds(row, 1)]), onehot(node_codes[pl.ds(row + 1, 1)])
            both = lax.dot_general(
                jnp.concatenate([tile_a, tile_b], 1),
                jnp.concatenate([jnp.concatenate([node_a, blank], 1), jnp.concatenate([blank, node_b], 1)], 0),
                NT,
                preferred_element_type=F32,
            )
            rows = jnp.concatenate([both[:, :128].reshape(16, 8, 128), both[:, 128:].reshape(16, 8, 128)], 1).astype(BF)
            for tile in range(16):
                adjacency[slot, tile // 2, pair * 16:pair * 16 + 16, tile % 2 * 128:tile % 2 * 128 + 128] = rows[tile]

    def multiply(block, slot):
        total = jnp.zeros((192, 128), F32)
        for pair in range(8):
            entry = group * 512 + (where[2] * 8 + block) * 16 + pair * 2
            halves = []
            for half in range(2):
                start = pl.multiple_of(tiles[entry + half] * 128, 128)
                halves.append(jnp.concatenate([ref[:, pl.ds(start, 128)] for ref in (f0, f1, f2, f3)], 0))
            total += lax.dot_general(jnp.concatenate(halves, 1), adjacency[slot, pair], NT, preferred_element_type=F32)
        out[0, :, pl.ds(pl.multiple_of(block * 128, 128), 128)] = total.astype(BF)

    def body(turn, unused):
        for at in range(4):
            build(turn * 4 + at, at)
        for at in range(4):
            multiply(turn * 4 + at, at)
        return 0

    lax.fori_loop(0, 2, body, 0)


def neighbour_sums(where, tiles, slots, counts, feats):
    whole = pl.BlockSpec((48, 16384), lambda i, where, tiles: (0, 0))
    return pl.pallas_call(
        sum_kernel,
        grid_spec=pltpu.PrefetchScalarGridSpec(
            num_scalar_prefetch=2,
            grid=(8,),
            in_specs=[
                pl.BlockSpec((1, 1, 16, 1024), lambda i, where, tiles: (group_at(i, where), 0, 0, where[2])),
                pl.BlockSpec((1, 8, 1024), lambda i, where, tiles: (group_at(i, where), 0, where[2])),
                whole, whole, whole, whole,
            ],
            out_specs=pl.BlockSpec((1, 192, 1024), lambda i, where, tiles: (i, 0, 0)),
            scratch_shapes=[
                pltpu.VMEM((128, 128), jnp.int32),
                pltpu.VMEM((128, 128), jnp.int32),
                pltpu.VMEM((4, 8, 128, 256), BF),
            ],
        ),
        out_shape=jax.ShapeDtypeStruct((8, 192, 1024), BF),
        compiler_params=pltpu.CompilerParams(vmem_limit_bytes=48 << 20),
    )(where, tiles, slots, counts, *feats)


def per_device(features, sampled_slots, block_index, counts, weight, cotangent):
    feat, batch = lax.axis_index("feat"), lax.axis_index("batch")
    z, y, x, core = feat // 4, feat % 4, batch // 2, batch % 2
    where = jnp.stack([x, core, z]).astype(jnp.int32)

    def around_z(array):
        return [array] + [along_z(array, -step) for step in (1, 2, 3)]

    sums = neighbour_sums(where, block_index.reshape(-1), sampled_slots, counts, around_z(features))
    mine = sums[4:].astype(F32) + flip(sums[:4], 1).astype(F32)
    mine_bf = mine.astype(BF)
    summed = mine[0]
    for step in (1, 2, 3):
        summed = summed + along_x(mine_bf[step], step).astype(F32)
    own_counts = lax.dynamic_slice(counts, (batch, 0, z * 1024), (1, 8, 1024))[0]
    totals = jnp.sum(own_counts, axis=0).astype(F32)
    aggregate = (summed / totals[None, :]).astype(BF)
    weights = jnp.concatenate(around_z(weight), 0)

    def rows_of(step):
        return lax.dynamic_slice(aggregate, (0, (y + step) % 4 * 256), (192, 256))

    rows = [rows_of(step) for step in range(4)]
    parts = [jnp.einsum("dr,dh->rh", block, weights, preferred_element_type=F32) for block in rows]
    preact = parts[0]
    for step in (1, 2, 3):
        preact = preact + along_y(parts[step].astype(BF), step).astype(F32)
    sigmoid_val = jax.nn.sigmoid(preact)
    hidden = (preact * sigmoid_val).astype(BF)
    pre_grad = (cotangent.astype(F32) * sigmoid_val * (1.0 + preact * (1.0 - sigmoid_val))).astype(BF)
    grad = jnp.dot(rows[0], pre_grad, preferred_element_type=F32)
    for step in (1, 2, 3):
        grad = grad + jnp.dot(rows[step], along_y(pre_grad, -step), preferred_element_type=F32)
    grad = grad.reshape(4, 48, 1024)
    weight_grad = grad[0]
    for step in (1, 2, 3):
        weight_grad = weight_grad + along_z(grad[step], step)
    for bit in (1, 2, 4):
        weight_grad = weight_grad + flip(weight_grad, bit)
    return hidden, weight_grad


def solution(mesh):
    placed = (
        P("feat", "batch"),
        P(None, "batch", None, None),
        P(None, "batch", None, None),
        P(),
        P("feat", None),
        P(("feat", "batch"), None),
    )
    return jax.shard_map(
        per_device,
        mesh=mesh,
        in_specs=placed,
        out_specs=(P(("feat", "batch"), None), P("feat", None)),
        check_vma=False,
    )
```

time: 1330 us -> 243 us (0.18)
  other arithmetic: 787 us -> 3.9 us
  matrix products: 158 us -> 4.75 us
  waiting for transfers between devices: 283 us -> 146 us
  local copies, waits for them, and re-layouts: 83 us -> 9.17 us
  Pallas kernels: 0 us -> 46.3 us
  starting transfers between devices: 0.16 us -> 30.8 us
    reduce_sum x17 -> x1, other arithmetic: 784 us -> 0.77 us  [per_device(): totals = jnp.sum(own_counts, axis=0).astype(F32)]
    reduce_scatter x2 -> x0, waiting for transfers between devices: 155 us -> none  [the longest x1 111 us: per_device(): lax.psum_scatter(jnp.einsum('dr,dh->rh', picked, weight, preferred_elemen...]
    dot_general x18 -> x8, matrix products: 158 us -> 4.75 us  [the longest x4 3.67 us: per_device(): jnp.einsum('dr,dh->rh', block, weights, preferred_element_type=F32)]
    ppermute x0 -> x22, waiting for transfers between devices: none -> 146 us  [shift(): return lax.ppermute(array, axis, [(at, move(at)) for at in range(size)])]
    all_gather x1 -> x0, waiting for transfers between devices: 70.7 us -> none  [per_device(): lax.all_gather(pre_grad, 'feat', axis=0, tiled=True)]
    psum x1 -> x0, waiting for transfers between devices: 57.2 us -> none  [per_device(): weight_grad = lax.psum(grad_part, 'batch')]
    pallas_call x0 -> x1, Pallas kernels: none -> 46.3 us  [neighbour_sums(): pl.pallas_call(sum_kernel, grid_spec=pltpu.PrefetchScalarGridSpec(num_sca...]
    gather x16 -> x0, local copies, waits for them, and re-layouts: 42.6 us -> none  [rowblock_sum(): gathered = jnp.take(blocks, tile_ids, axis=1).reshape(feat_width, tile_span)]
  transfers between devices with their start and end apart: 4 -> 22, of which waited for: 4 -> 16; matrix products, arithmetic and copies ran while one was open for 0% -> 3% of each run, Pallas kernels for 0% -> 0%
where the time goes in v1:
time: 243 us; the launch traced here: 241 us
  waiting for transfers between devices  146 us (60%)
  Pallas kernels  46.3 us (19%)
  starting transfers between devices  30.8 us (13%)
  local copies, waits for them, and re-layouts  9.17 us (4%)
  matrix products  4.75 us (2%)
  other arithmetic  3.9 us (2%)
    ppermute x22, waiting for transfers between devices, shift(): return lax.ppermute(array, axis, [(at, move(at)) for at in range(size)])  146 us
    pallas_call x1, Pallas kernels, neighbour_sums(): pl.pallas_call(sum_kernel, grid_spec=pltpu.PrefetchScalarGridSpec(num_sca...  46.3 us
    ppermute x22, starting transfers between devices, shift(): return lax.ppermute(array, axis, [(at, move(at)) for at in range(size)])  30.8 us
    unnamed x16, local copies, waits for them, and re-layouts  6.28 us
  transfers between devices with their start and end apart: 22, of which 16 were waited for; matrix products, arithmetic and copies ran while one was open for 3% of the time, Pallas kernels for 0%

profile of v1, /device:TPU:1, one launch (start us, length us, event | category | flops | bytes accessed | tf_op | source)
XLA Modules:
  0.0 241.3 jit_solution(16953287506273266957)
XLA Ops:
  0.6 4.7 %collective-permute-start = (bf16[48,16384]{1,0:T(8,128)(2,1)}, bf16[48,16384]{1,0:T(8,128)(2,1)S(1)}, u32[]{:S(2)}, u32[]{:S(2)}) collective-permute-start(bf16[48,16384]{1,0:T(8,128)(2,1)} %f0.1), channel_id=1, source_target_pairs={{0,96},{8,104},{16,112},{24,120},{32,0},{40,8},{48,16},{56,24},{64... | collective-permute-start | bytes 4718600 | tf_op jit(solution)/shard_map/ppermute | solution.py:15
  5.3 0.0 collective-permute-start.1
  5.3 0.7 collective-permute-start.2
  6.0 0.9 copy.8
  6.9 0.1 reshape.19.tiles
  7.0 0.1 pad_add_fusion.where
  7.1 65.1 %collective-permute-done.f1 = bf16[48,16384]{1,0:T(8,128)(2,1)S(1)} collective-permute-done((bf16[48,16384]{1,0:T(8,128)(2,1)}, bf16[48,16384]{1,0:T(8,128)(2,1)S(1)}, u32[]{:S(2)}, u32[]{:S(2)}) %collective-permute-start) | collective-permute-done | bytes 1572896 | tf_op jit(solution)/shard_map/ppermute | solution.py:15
  72.2 4.3 %collective-permute-done.2.f3 = bf16[48,16384]{1,0:T(8,128)(2,1)} collective-permute-done((bf16[48,16384]{1,0:T(8,128)(2,1)}, bf16[48,16384]{1,0:T(8,128)(2,1)}, u32[]{:S(2)}, u32[]{:S(2)}) %collective-permute-start.2) | collective-permute-done | bytes 1572896 | tf_op jit(solution)/shard_map/ppermute | solution.py:15
  76.5 1.4 copy-done
  77.9 1.2 copy-done.1
  79.1 46.3 %shard_map.77 = bf16[8,192,1024]{2,1,0:T(8,128)(2,1)} custom-call(s32[3]{0:T(128)S(1)} %pad_add_fusion.where, s32[4096]{0:T(1024)S(1)} %reshape.19.tiles, s32[8,1,16,4096]{3,2,1,0:T(8,128)} %slots.1, s32[8,8,4096]{2,1,0:T(8,128)S(1)} %copy-done.1, bf16[48,16384]{1,0:T(8,128)(2,1)S(1)} %copy-done, bf16[48,16384]{1,0:T(8,128)(2,1)S(1)} %collective-permute-done.f1, ...), custom_call_target="tpu_custom_call" | custom-call | tf_op jit(solution)/shard_map/pallas_call | solution.py:110
  125.4 1.7 slice.45
  127.1 0.9 collective-permute-start.3
  128.0 0.7 collective-permute-start.7
  128.7 2.4 collective-permute-done.3
  131.1 0.8 convert_add_fusion
  131.9 1.0 slice_bitcast_fusion.3
  132.9 1.2 collective-permute-start.4
  134.1 2.5 %collective-permute-start.5 = (bf16[192,1024]{1,0:T(8,128)(2,1)}, bf16[192,1024]{1,0:T(8,128)(2,1)}, u32[]{:S(2)}, u32[]{:S(2)}) collective-permute-start(bf16[192,1024]{1,0:T(8,128)(2,1)} %get-tuple-element.6), channel_id=1, source_target_pairs={{0,4},{1,5},{2,6},{3,7},{4,0},{5,1},{6,2},{7,3},{8,12},{9,13},{10,... | collective-permute-start | bytes 1179656 | tf_op jit(solution)/shard_map/ppermute | solution.py:15
  136.6 1.1 collective-permute-start.6
  137.7 0.9 constant_dynamic-update-slice_fusion.3
  138.6 0.8 dynamic-slice_reduce_fusion
  139.5 0.1 collective-permute-start.9
  139.5 0.9 constant_dynamic-update-slice_fusion.2
  140.4 0.0 collective-permute-done.8
  140.4 0.9 constant_dynamic-update-slice_fusion.1
  141.3 3.5 %collective-permute-done.9 = bf16[48,1024]{1,0:T(8,128)(2,1)S(1)} collective-permute-done((bf16[48,1024]{1,0:T(8,128)(2,1)}, bf16[48,1024]{1,0:T(8,128)(2,1)S(1)}, u32[]{:S(2)}, u32[]{:S(2)}) %collective-permute-start.9) | collective-permute-done | bytes 98336 | tf_op jit(solution)/shard_map/ppermute | solution.py:15
  144.8 0.0 collective-permute-done.4
  144.8 9.4 %collective-permute-done.5 = bf16[192,1024]{1,0:T(8,128)(2,1)} collective-permute-done((bf16[192,1024]{1,0:T(8,128)(2,1)}, bf16[192,1024]{1,0:T(8,128)(2,1)}, u32[]{:S(2)}, u32[]{:S(2)}) %collective-permute-start.5) | collective-permute-done | bytes 393248 | tf_op jit(solution)/shard_map/ppermute | solution.py:15
  154.2 1.5 fusion.7
  155.7 0.0 copy-start.5
  155.7 0.3 convolution_convert_fusion.2
  156.0 1.4 collective-permute-start.10
  157.4 0.3 convolution_convert_fusion.1
  157.7 2.7 %collective-permute-start.11 = (bf16[256,1024]{1,0:T(8,128)(2,1)S(1)}, bf16[256,1024]{1,0:T(8,128)(2,1)S(1)}, u32[]{:S(2)}, u32[]{:S(2)}) collective-permute-start(bf16[256,1024]{1,0:T(8,128)(2,1)S(1)} %convolution_convert_fusion.1), channel_id=1, source_target_pairs={{0,16},{8,24},{16,0},{24,8},{32,48},{40,56},{48,32},{56,40},{64,80... | collective-permute-start | bytes 1572872 | tf_op jit(solution)/shard_map/ppermute | solution.py:15
  160.4 0.3 convolution_convert_fusion
  160.8 1.1 collective-permute-start.12
  161.9 7.7 %collective-permute-done.10 = bf16[256,1024]{1,0:T(8,128)(2,1)S(1)} collective-permute-done((bf16[256,1024]{1,0:T(8,128)(2,1)S(1)}, bf16[256,1024]{1,0:T(8,128)(2,1)S(1)}, u32[]{:S(2)}, u32[]{:S(2)}) %collective-permute-start.10) | collective-permute-done | bytes 524320 | tf_op jit(solution)/shard_map/ppermute | solution.py:15
  169.6 12.4 %collective-permute-done.11 = bf16[256,1024]{1,0:T(8,128)(2,1)S(1)} collective-permute-done((bf16[256,1024]{1,0:T(8,128)(2,1)S(1)}, bf16[256,1024]{1,0:T(8,128)(2,1)S(1)}, u32[]{:S(2)}, u32[]{:S(2)}) %collective-permute-start.11) | collective-permute-done | bytes 524320 | tf_op jit(solution)/shard_map/ppermute | solution.py:15
  182.0 0.4 collective-permute-done.12
  182.4 2.7 %multiply_convert_fusion = (bf16[256,1024]{1,0:T(8,128)(2,1)S(1)}, bf16[256,1024]{1,0:T(8,128)(2,1)}) fusion(bf16[256,1024]{1,0:T(8,128)(2,1)S(1)} %copy-done.5, bf16[256,1024]{1,0:T(8,128)(2,1)} %collective-permute-done.12, bf16[256,1024]{1,0:T(8,128)(2,1)S(1)} %collective-permute-done.11, bf16[256,1024]{1,0:T(8,128)(2,1)S(1)} %collective-permute-done.10, ...), kind=kOutput, calls=%fused_computation.10 | convolution fusion | flops 105381888 | bytes 3637252 | tf_op jit(solution)/shard_map/dr,dh->rh/dot_general | solution.py:155
  185.1 2.6 %collective-permute-start.15 = (bf16[256,1024]{1,0:T(8,128)(2,1)S(1)}, bf16[256,1024]{1,0:T(8,128)(2,1)S(1)}, u32[]{:S(2)}, u32[]{:S(2)}) collective-permute-start(bf16[256,1024]{1,0:T(8,128)(2,1)S(1)} %get-tuple-element.7), channel_id=1, source_target_pairs={{0,8},{8,16},{16,24},{24,0},{32,40},{40,48},{48,56},{56,32},{64,72... | collective-permute-start | bytes 1572872 | tf_op jit(solution)/shard_map/ppermute | solution.py:15
  187.7 1.0 collective-permute-start.13
  188.7 1.2 collective-permute-start.14
  189.8 0.3 fusion.17
  190.1 9.7 %collective-permute-done.15 = bf16[256,1024]{1,0:T(8,128)(2,1)S(1)} collective-permute-done((bf16[256,1024]{1,0:T(8,128)(2,1)S(1)}, bf16[256,1024]{1,0:T(8,128)(2,1)S(1)}, u32[]{:S(2)}, u32[]{:S(2)}) %collective-permute-start.15) | collective-permute-done | bytes 524320 | tf_op jit(solution)/shard_map/ppermute | solution.py:15
  199.8 0.3 fusion.10
  200.1 0.3 convolution_add_fusion.2
  200.3 12.3 %collective-permute-done.14 = bf16[256,1024]{1,0:T(8,128)(2,1)S(1)} collective-permute-done((bf16[256,1024]{1,0:T(8,128)(2,1)S(1)}, bf16[256,1024]{1,0:T(8,128)(2,1)S(1)}, u32[]{:S(2)}, u32[]{:S(2)}) %collective-permute-start.14) | collective-permute-done | bytes 524320 | tf_op jit(solution)/shard_map/ppermute | solution.py:15
  212.6 0.3 fusion.2
  212.9 0.1 collective-permute-start.16
  213.0 1.7 collective-permute-start.17
  214.7 1.0 collective-permute-start.18
  215.7 5.0 %collective-permute-done.16 = f32[48,1024]{1,0:T(8,128)S(1)} collective-permute-done((f32[48,1024]{1,0:T(8,128)S(1)}, f32[48,1024]{1,0:T(8,128)S(1)}, u32[]{:S(2)}, u32[]{:S(2)}) %collective-permute-start.16) | collective-permute-done | bytes 196640 | tf_op jit(solution)/shard_map/ppermute | solution.py:15
  220.6 1.8 collective-permute-done.17
  222.5 1.5 collective-permute-done.18
  224.0 0.1 fusion.9
  224.1 2.4 %collective-permute-start.19 = (f32[48,1024]{1,0:T(8,128)S(1)}, f32[48,1024]{1,0:T(8,128)S(1)}, u32[]{:S(2)}, u32[]{:S(2)}) collective-permute-start(f32[48,1024]{1,0:T(8,128)S(1)} %fusion.9), channel_id=1, source_target_pairs={{0,1},{1,0},{2,3},{3,2},{4,5},{5,4},{6,7},{7,6},{8,9},{9,8},{10,11... | collective-permute-start | bytes 589832 | tf_op jit(solution)/shard_map/ppermute | solution.py:15
  226.5 1.1 collective-permute-done.19
  227.6 1.1 collective-permute-start.20
  228.7 5.1 %collective-permute-done.20 = f32[48,1024]{1,0:T(8,128)S(1)} collective-permute-done((f32[48,1024]{1,0:T(8,128)S(1)}, f32[48,1024]{1,0:T(8,128)S(1)}, u32[]{:S(2)}, u32[]{:S(2)}) %collective-permute-start.20) | collective-permute-done | bytes 196640 | tf_op jit(solution)/shard_map/ppermute | solution.py:15
  233.8 2.8 %collective-permute-start.21 = (f32[48,1024]{1,0:T(8,128)S(1)}, f32[48,1024]{1,0:T(8,128)S(1)}, u32[]{:S(2)}, u32[]{:S(2)}) collective-permute-start(f32[48,1024]{1,0:T(8,128)S(1)} %add.133), channel_id=1, source_target_pairs={{0,4},{1,5},{2,6},{3,7},{4,0},{5,1},{6,2},{7,3},{8,12},{9,13},{10,... | collective-permute-start | bytes 589832 | tf_op jit(solution)/shard_map/ppermute | solution.py:15
  236.6 4.0 %collective-permute-done.21 = f32[48,1024]{1,0:T(8,128)S(1)} collective-permute-done((f32[48,1024]{1,0:T(8,128)S(1)}, f32[48,1024]{1,0:T(8,128)S(1)}, u32[]{:S(2)}, u32[]{:S(2)}) %collective-permute-start.21) | collective-permute-done | bytes 196640 | tf_op jit(solution)/shard_map/ppermute | solution.py:15
  240.6 0.7 add.134
  (19 shorter events, 0.1 us)
Async XLA Ops:
  0.6 71.6 %collective-permute-start = (bf16[48,16384]{1,0:T(8,128)(2,1)}, bf16[48,16384]{1,0:T(8,128)(2,1)S(1)}, u32[]{:S(2)}, u32[]{:S(2)}) collective-permute-start(bf16[48,16384]{1,0:T(8,128)(2,1)} %f0.1), channel_id=1, source_target_pairs={{0,96},{8,104},{16,112},{24,120},{32,0},{40,8},{48,16},{56,24},{64... | collective-permute-start | bytes 4718600 | tf_op jit(solution)/shard_map/ppermute | solution.py:15
  5.3 66.9 %collective-permute-start.1 = (bf16[48,16384]{1,0:T(8,128)(2,1)}, bf16[48,16384]{1,0:T(8,128)(2,1)S(1)}, u32[]{:S(2)}, u32[]{:S(2)}) collective-permute-start(bf16[48,16384]{1,0:T(8,128)(2,1)} %f0.1), channel_id=1, source_target_pairs={{0,64},{8,72},{16,80},{24,88},{32,96},{40,104},{48,112},{56,120},{... | collective-permute-start | bytes 4718600 | tf_op jit(solution)/shard_map/ppermute | solution.py:15
  5.3 71.2 %collective-permute-start.2 = (bf16[48,16384]{1,0:T(8,128)(2,1)}, bf16[48,16384]{1,0:T(8,128)(2,1)}, u32[]{:S(2)}, u32[]{:S(2)}) collective-permute-start(bf16[48,16384]{1,0:T(8,128)(2,1)} %f0.1), channel_id=1, source_target_pairs={{0,32},{8,40},{16,48},{24,56},{32,64},{40,72},{48,80},{56,88},{64,... | collective-permute-start | bytes 4718600 | tf_op jit(solution)/shard_map/ppermute | solution.py:15
  76.5 1.4 copy-start
  77.9 1.2 copy-start.1
  125.4 5.7 %copy-start.2 = (bf16[8,192,1024]{2,1,0:T(8,128)(2,1)S(1)}, bf16[8,192,1024]{2,1,0:T(8,128)(2,1)}, u32[]{:S(2)}) copy-start(bf16[8,192,1024]{2,1,0:T(8,128)(2,1)} %shard_map.77) | copy-start | bytes 9437188
  127.1 3.9 %collective-permute-start.3 = (bf16[4,192,1024]{2,1,0:T(8,128)(2,1)S(1)}, bf16[4,192,1024]{2,1,0:T(8,128)(2,1)S(1)}, u32[]{:S(2)}, u32[]{:S(2)}) collective-permute-start(bf16[4,192,1024]{2,1,0:T(8,128)(2,1)S(1)} %slice.45), channel_id=1, source_target_pairs={{0,1},{1,0},{2,3},{3,2},{4,5},{5,4},{6,7},{7,6},{8,9},{9,8},{10,11... | collective-permute-start | bytes 4718600 | tf_op jit(solution)/shard_map/ppermute | solution.py:15
  128.0 11.4 %collective-permute-start.7 = (bf16[48,1024]{1,0:T(8,128)(2,1)}, bf16[48,1024]{1,0:T(8,128)(2,1)}, u32[]{:S(2)}, u32[]{:S(2)}) collective-permute-start(bf16[48,1024]{1,0:T(8,128)(2,1)} %param.10), channel_id=1, source_target_pairs={{0,96},{8,104},{16,112},{24,120},{32,0},{40,8},{48,16},{56,24},{64... | collective-permute-start | bytes 294920 | tf_op jit(solution)/shard_map/ppermute | solution.py:15
  128.7 11.7 %collective-permute-start.8 = (bf16[48,1024]{1,0:T(8,128)(2,1)}, bf16[48,1024]{1,0:T(8,128)(2,1)}, u32[]{:S(2)}, u32[]{:S(2)}) collective-permute-start(bf16[48,1024]{1,0:T(8,128)(2,1)} %param.10), channel_id=1, source_target_pairs={{0,64},{8,72},{16,80},{24,88},{32,96},{40,104},{48,112},{56,120},{... | collective-permute-start | bytes 294920 | tf_op jit(solution)/shard_map/ppermute | solution.py:15
  132.9 11.9 %collective-permute-start.4 = (bf16[192,1024]{1,0:T(8,128)(2,1)}, bf16[192,1024]{1,0:T(8,128)(2,1)}, u32[]{:S(2)}, u32[]{:S(2)}) collective-permute-start(bf16[192,1024]{1,0:T(8,128)(2,1)} %get-tuple-element.4), channel_id=1, source_target_pairs={{0,2},{1,3},{2,4},{3,5},{4,6},{5,7},{6,0},{7,1},{8,10},{9,11},{10,... | collective-permute-start | bytes 1179656 | tf_op jit(solution)/shard_map/ppermute | solution.py:15
  134.1 20.1 %collective-permute-start.5 = (bf16[192,1024]{1,0:T(8,128)(2,1)}, bf16[192,1024]{1,0:T(8,128)(2,1)}, u32[]{:S(2)}, u32[]{:S(2)}) collective-permute-start(bf16[192,1024]{1,0:T(8,128)(2,1)} %get-tuple-element.6), channel_id=1, source_target_pairs={{0,4},{1,5},{2,6},{3,7},{4,0},{5,1},{6,2},{7,3},{8,12},{9,13},{10,... | collective-permute-start | bytes 1179656 | tf_op jit(solution)/shard_map/ppermute | solution.py:15
  136.6 17.6 %collective-permute-start.6 = (bf16[192,1024]{1,0:T(8,128)(2,1)}, bf16[192,1024]{1,0:T(8,128)(2,1)}, u32[]{:S(2)}, u32[]{:S(2)}) collective-permute-start(bf16[192,1024]{1,0:T(8,128)(2,1)} %get-tuple-element.5), channel_id=1, source_target_pairs={{0,6},{1,7},{2,0},{3,1},{4,2},{5,3},{6,4},{7,5},{8,14},{9,15},{10,... | collective-permute-start | bytes 1179656 | tf_op jit(solution)/shard_map/ppermute | solution.py:15
  139.5 5.4 %collective-permute-start.9 = (bf16[48,1024]{1,0:T(8,128)(2,1)}, bf16[48,1024]{1,0:T(8,128)(2,1)S(1)}, u32[]{:S(2)}, u32[]{:S(2)}) collective-permute-start(bf16[48,1024]{1,0:T(8,128)(2,1)} %param.10), channel_id=1, source_target_pairs={{0,32},{8,40},{16,48},{24,56},{32,64},{40,72},{48,80},{56,88},{64,... | collective-permute-start | bytes 294920 | tf_op jit(solution)/shard_map/ppermute | solution.py:15
  155.7 4.8 %copy-start.3 = (bf16[192,1024]{1,0:T(8,128)(2,1)}, bf16[192,1024]{1,0:T(8,128)(2,1)S(1)}, u32[]{:S(2)}) copy-start(bf16[192,1024]{1,0:T(8,128)(2,1)S(1)} %fusion.7) | copy-start | bytes 1179652
  155.7 26.8 %copy-start.5 = (bf16[256,1024]{1,0:T(8,128)(2,1)S(1)}, bf16[256,1024]{1,0:T(8,128)(2,1)}, u32[]{:S(2)}) copy-start(bf16[256,1024]{1,0:T(8,128)(2,1)} %param.11) | copy-start | bytes 1572868
  156.0 13.6 %collective-permute-start.10 = (bf16[256,1024]{1,0:T(8,128)(2,1)S(1)}, bf16[256,1024]{1,0:T(8,128)(2,1)S(1)}, u32[]{:S(2)}, u32[]{:S(2)}) collective-permute-start(bf16[256,1024]{1,0:T(8,128)(2,1)S(1)} %convolution_convert_fusion.2), channel_id=1, source_target_pairs={{0,8},{8,16},{16,24},{24,0},{32,40},{40,48},{48,56},{56,32},{64,72... | collective-permute-start | bytes 1572872 | tf_op jit(solution)/shard_map/ppermute | solution.py:15
  157.7 24.3 %collective-permute-start.11 = (bf16[256,1024]{1,0:T(8,128)(2,1)S(1)}, bf16[256,1024]{1,0:T(8,128)(2,1)S(1)}, u32[]{:S(2)}, u32[]{:S(2)}) collective-permute-start(bf16[256,1024]{1,0:T(8,128)(2,1)S(1)} %convolution_convert_fusion.1), channel_id=1, source_target_pairs={{0,16},{8,24},{16,0},{24,8},{32,48},{40,56},{48,32},{56,40},{64,80... | collective-permute-start | bytes 1572872 | tf_op jit(solution)/shard_map/ppermute | solution.py:15
  160.8 21.7 %collective-permute-start.12 = (bf16[256,1024]{1,0:T(8,128)(2,1)S(1)}, bf16[256,1024]{1,0:T(8,128)(2,1)}, u32[]{:S(2)}, u32[]{:S(2)}) collective-permute-start(bf16[256,1024]{1,0:T(8,128)(2,1)S(1)} %convolution_convert_fusion), channel_id=1, source_target_pairs={{0,24},{8,0},{16,8},{24,16},{32,56},{40,32},{48,40},{56,48},{64,88... | collective-permute-start | bytes 1572872 | tf_op jit(solution)/shard_map/ppermute | solution.py:15
  161.9 27.9 %copy-start.4 = (bf16[192,1024]{1,0:T(8,128)(2,1)S(1)}, bf16[192,1024]{1,0:T(8,128)(2,1)}, u32[]{:S(2)}) copy-start(bf16[192,1024]{1,0:T(8,128)(2,1)} %copy-done.3) | copy-start | bytes 1179652
  185.1 14.6 %collective-permute-start.15 = (bf16[256,1024]{1,0:T(8,128)(2,1)S(1)}, bf16[256,1024]{1,0:T(8,128)(2,1)S(1)}, u32[]{:S(2)}, u32[]{:S(2)}) collective-permute-start(bf16[256,1024]{1,0:T(8,128)(2,1)S(1)} %get-tuple-element.7), channel_id=1, source_target_pairs={{0,8},{8,16},{16,24},{24,0},{32,40},{40,48},{48,56},{56,32},{64,72... | collective-permute-start | bytes 1572872 | tf_op jit(solution)/shard_map/ppermute | solution.py:15
  187.7 12.4 %collective-permute-start.13 = (bf16[256,1024]{1,0:T(8,128)(2,1)S(1)}, bf16[256,1024]{1,0:T(8,128)(2,1)S(1)}, u32[]{:S(2)}, u32[]{:S(2)}) collective-permute-start(bf16[256,1024]{1,0:T(8,128)(2,1)S(1)} %get-tuple-element.7), channel_id=1, source_target_pairs={{0,24},{8,0},{16,8},{24,16},{32,56},{40,32},{48,40},{56,48},{64,88... | collective-permute-start | bytes 1572872 | tf_op jit(solution)/shard_map/ppermute | solution.py:15
  188.7 23.9 %collective-permute-start.14 = (bf16[256,1024]{1,0:T(8,128)(2,1)S(1)}, bf16[256,1024]{1,0:T(8,128)(2,1)S(1)}, u32[]{:S(2)}, u32[]{:S(2)}) collective-permute-start(bf16[256,1024]{1,0:T(8,128)(2,1)S(1)} %get-tuple-element.7), channel_id=1, source_target_pairs={{0,16},{8,24},{16,0},{24,8},{32,48},{40,56},{48,32},{56,40},{64,80... | collective-permute-start | bytes 1572872 | tf_op jit(solution)/shard_map/ppermute | solution.py:15
  212.9 7.7 %collective-permute-start.16 = (f32[48,1024]{1,0:T(8,128)S(1)}, f32[48,1024]{1,0:T(8,128)S(1)}, u32[]{:S(2)}, u32[]{:S(2)}) collective-permute-start(f32[48,1024]{1,0:T(8,128)S(1)} %get-tuple-element.9), channel_id=1, source_target_pairs={{0,32},{8,40},{16,48},{24,56},{32,64},{40,72},{48,80},{56,88},{64,... | collective-permute-start | bytes 589832 | tf_op jit(solution)/shard_map/ppermute | solution.py:15
  213.0 9.5 %collective-permute-start.17 = (f32[48,1024]{1,0:T(8,128)S(1)}, f32[48,1024]{1,0:T(8,128)S(1)}, u32[]{:S(2)}, u32[]{:S(2)}) collective-permute-start(f32[48,1024]{1,0:T(8,128)S(1)} %get-tuple-element.11), channel_id=1, source_target_pairs={{0,64},{8,72},{16,80},{24,88},{32,96},{40,104},{48,112},{56,120},{... | collective-permute-start | bytes 589832 | tf_op jit(solution)/shard_map/ppermute | solution.py:15
  214.7 9.3 %collective-permute-start.18 = (f32[48,1024]{1,0:T(8,128)S(1)}, f32[48,1024]{1,0:T(8,128)S(1)}, u32[]{:S(2)}, u32[]{:S(2)}) collective-permute-start(f32[48,1024]{1,0:T(8,128)S(1)} %get-tuple-element.10), channel_id=1, source_target_pairs={{0,96},{8,104},{16,112},{24,120},{32,0},{40,8},{48,16},{56,24},{64... | collective-permute-start | bytes 589832 | tf_op jit(solution)/shard_map/ppermute | solution.py:15
  224.1 3.5 %collective-permute-start.19 = (f32[48,1024]{1,0:T(8,128)S(1)}, f32[48,1024]{1,0:T(8,128)S(1)}, u32[]{:S(2)}, u32[]{:S(2)}) collective-permute-start(f32[48,1024]{1,0:T(8,128)S(1)} %fusion.9), channel_id=1, source_target_pairs={{0,1},{1,0},{2,3},{3,2},{4,5},{5,4},{6,7},{7,6},{8,9},{9,8},{10,11... | collective-permute-start | bytes 589832 | tf_op jit(solution)/shard_map/ppermute | solution.py:15
  227.6 6.2 %collective-permute-start.20 = (f32[48,1024]{1,0:T(8,128)S(1)}, f32[48,1024]{1,0:T(8,128)S(1)}, u32[]{:S(2)}, u32[]{:S(2)}) collective-permute-start(f32[48,1024]{1,0:T(8,128)S(1)} %add.132), channel_id=1, source_target_pairs={{0,2},{1,3},{2,0},{3,1},{4,6},{5,7},{6,4},{7,5},{8,10},{9,11},{10,... | collective-permute-start | bytes 589832 | tf_op jit(solution)/shard_map/ppermute | solution.py:15
  233.8 6.8 %collective-permute-start.21 = (f32[48,1024]{1,0:T(8,128)S(1)}, f32[48,1024]{1,0:T(8,128)S(1)}, u32[]{:S(2)}, u32[]{:S(2)}) collective-permute-start(f32[48,1024]{1,0:T(8,128)S(1)} %add.133), channel_id=1, source_target_pairs={{0,4},{1,5},{2,6},{3,7},{4,0},{5,1},{6,2},{7,3},{8,12},{9,13},{10,... | collective-permute-start | bytes 589832 | tf_op jit(solution)/shard_map/ppermute | solution.py:15

commit v2 on v1

v2 whole, which is shorter than its diff:
```python
import jax
import jax.numpy as jnp
from jax import lax
from jax.experimental import pallas as pl
from jax.experimental.pallas import tpu as pltpu
from jax.sharding import PartitionSpec as P

BF = jnp.bfloat16
F32 = jnp.float32
NT = (((1,), (1,)), ((), ()))


def shift(array, axis, move):
    size = lax.axis_size(axis)
    return lax.ppermute(array, axis, [(at, move(at)) for at in range(size)])


def along_z(array, step):
    return shift(array, "feat", lambda at: (at + 4 * step) % 16)


def along_y(array, step):
    return shift(array, "feat", lambda at: at // 4 * 4 + (at + step) % 4)


def flip(array, bit):
    return shift(array, "batch", lambda at: at ^ bit)


def edge_codes(slots, used):
    slot_row = lax.broadcasted_iota(jnp.int32, slots.shape, 0) & 15
    lane = lax.broadcasted_iota(jnp.int32, slots.shape, 1)
    height = slots.shape[0]
    value = jnp.where(slot_row < used, slots, -1)
    for bit in range(4):
        rows, lanes = 1 << bit, 8 << bit
        row_bit = (slot_row >> bit) & 1
        lane_bit = (lane >> (bit + 3)) & 1
        later = pltpu.roll(pltpu.roll(value, height - rows, 0), lanes, 1)
        earlier = pltpu.roll(pltpu.roll(value, rows, 0), 128 - lanes, 1)
        value = jnp.where(row_bit < lane_bit, later, jnp.where(row_bit > lane_bit, earlier, value))
    return (value >> 7) * 8 + (lane & 7), value & 127


def onehot(code):
    rows = lax.broadcasted_iota(jnp.int32, (128, 128), 0).astype(BF)
    match = jnp.broadcast_to(code.astype(BF), (128, 128)) == rows
    return jnp.where(match, BF(1), BF(0))


def group_at(step, where):
    return lax.rem(where[0] + 3 - step % 4, 4) * 2 + lax.rem(where[1] + 1 - step // 4, 2)


def build(adjacency, pairs_at, block, tile_codes, node_codes):
    blank = jnp.zeros((128, 128), BF)
    for pair in range(8):
        row = block * 16 + 2 * pair
        tile_a, tile_b = onehot(tile_codes[pl.ds(row, 1)]), onehot(tile_codes[pl.ds(row + 1, 1)])
        node_a, node_b = onehot(node_codes[pl.ds(row, 1)]), onehot(node_codes[pl.ds(row + 1, 1)])
        both = lax.dot_general(
            jnp.concatenate([tile_a, tile_b], 1),
            jnp.concatenate([jnp.concatenate([node_a, blank], 1), jnp.concatenate([blank, node_b], 1)], 0),
            NT,
            preferred_element_type=F32,
        )
        rows = jnp.concatenate([both[:, :128].reshape(16, 8, 128), both[:, 128:].reshape(16, 8, 128)], 1).astype(BF)
        for tile in range(16):
            adjacency[pairs_at, tile // 2, pair * 16:pair * 16 + 16, tile % 2 * 128:tile % 2 * 128 + 128] = rows[tile]


def remote(src, dst, sems, at, target):
    return pltpu.make_async_remote_copy(
        src_ref=src, dst_ref=dst, send_sem=sems.at[0, at], recv_sem=sems.at[1, at],
        device_id=target, device_id_type=pl.DeviceIdType.MESH,
    )


def sum_kernel(
    features, slots, counts, tiles, aggregate,
    raw, feats, slot_rows, used, tile_codes, node_codes, adjacency, core_out, core_in, x_out, x_in, own,
    load_sems, z_sems, core_sems, x_sems,
):
    feat, batch = lax.axis_index("feat"), lax.axis_index("batch")
    z, y, x, core = feat // 4, feat % 4, batch // 2, batch % 2
    where = (x, core)

    def z_at(step):
        return (lax.rem(z + step, 4) * 4 + y, batch)

    def x_at(step):
        return (feat, lax.rem(x + step, 4) * 2 + core)

    partner = (feat, x * 2 + 1 - core)
    barrier = pltpu.get_barrier_semaphore()
    for device in (z_at(1), z_at(3), partner, x_at(1), x_at(2), x_at(3)):
        pl.semaphore_signal(barrier, inc=1, device_id=device, device_id_type=pl.DeviceIdType.MESH)
    own_columns = pl.ds(pl.multiple_of(z * 1024, 1024), 1024)
    loads = [
        pltpu.make_async_copy(slots.at[:, 0, :, own_columns], slot_rows, load_sems.at[0]),
        pltpu.make_async_copy(counts.at[:, :, own_columns], used, load_sems.at[1]),
        pltpu.make_async_copy(features, raw, load_sems.at[2]),
    ]
    for load in loads:
        load.start()
    loads[2].wait()
    for tile in range(128):
        feats[tile, 0:48, :] = raw[:, tile * 128:tile * 128 + 128]
    pl.semaphore_wait(barrier, 6)

    low, high = pl.ds(0, 64), pl.ds(64, 64)

    def shard(at, tiles_of):
        return feats.at[tiles_of, pl.ds(48 * at, 48), :]

    ring = [
        remote(shard(0, low), shard(3, low), z_sems, 0, z_at(1)),
        remote(shard(0, high), shard(1, high), z_sems, 1, z_at(3)),
        remote(shard(0, high), shard(3, high), z_sems, 2, z_at(1)),
        remote(shard(0, low), shard(1, low), z_sems, 3, z_at(3)),
        remote(shard(3, low), shard(2, low), z_sems, 4, z_at(1)),
        remote(shard(1, high), shard(2, high), z_sems, 5, z_at(3)),
    ]
    ring[0].start()
    ring[1].start()
    loads[0].wait()
    loads[1].wait()

    def build_group(step, unused):
        group = group_at(step, where)
        group_used = used[group, pl.ds(batch, 1), :]
        tile_code, node_code = edge_codes(
            jnp.concatenate([slot_rows[group, :, b * 128:b * 128 + 128] for b in range(8)], 0),
            jnp.concatenate([jnp.broadcast_to(group_used[:, b * 128:b * 128 + 128], (16, 128)) for b in range(8)], 0),
        )
        tile_codes[...] = tile_code
        node_codes[...] = node_code

        def some(turn, unused):
            for at in range(4):
                build(adjacency, step * 8 + turn * 4 + at, turn * 4 + at, tile_codes, node_codes)
            return 0

        return lax.fori_loop(0, 2, some, 0)

    lax.fori_loop(0, 4, build_group, 0)
    ring[2].start()
    ring[3].start()
    lax.fori_loop(4, 6, build_group, 0)
    ring[0].wait_recv()
    ring[1].wait_recv()
    ring[4].start()
    ring[5].start()
    lax.fori_loop(6, 8, build_group, 0)
    for at in (2, 3, 4, 5):
        ring[at].wait_recv()
    for at in range(6):
        ring[at].wait_send()

    def products(step, put):
        group = group_at(step, where)

        def one(block):
            total = jnp.zeros((192, 128), F32)
            for pair in range(8):
                entry = (z * 8 + block) * 16 + pair * 2
                halves = [feats[tiles[group, entry + half]] for half in range(2)]
                total += lax.dot_general(
                    jnp.concatenate(halves, 1), adjacency[step * 8 + block, pair], NT, preferred_element_type=F32
                )
            put(pl.ds(pl.multiple_of(block * 128, 128), 128), total)

        def some(turn, unused):
            for at in range(4):
                one(turn * 4 + at)
            return 0

        lax.fori_loop(0, 2, some, 0)

    def core_copy(at):
        return remote(core_out.at[at], core_in.at[at], core_sems, at, partner)

    def x_copy(at):
        return remote(x_out.at[at], x_in.at[at], x_sems, at, x_at(3 - at))

    def for_partner(step, unused):
        def put(columns, total):
            core_out[step, :, columns] = total

        products(step, put)
        core_copy(step).start()
        return 0

    lax.fori_loop(0, 4, for_partner, 0)

    def for_x(at, unused):
        core_copy(at).wait_recv()

        def put(columns, total):
            x_out[at, :, columns] = (total + core_in[at, :, columns]).astype(BF)

        products(at + 4, put)
        x_copy(at).start()
        return 0

    lax.fori_loop(0, 3, for_x, 0)
    core_copy(3).wait_recv()

    def put_own(columns, total):
        own[:, columns] = total + core_in[3, :, columns]

    products(7, put_own)
    totals = jnp.sum(used[batch], axis=0, keepdims=True).astype(F32)
    for at in range(3):
        x_copy(at).wait_recv()
    for block in range(8):
        columns = slice(block * 128, block * 128 + 128)
        summed = own[:, columns]
        for at in range(3):
            summed = summed + x_in[at, :, columns].astype(F32)
        aggregate[:, columns] = (summed / totals[:, columns]).astype(BF)
    for at in range(4):
        core_copy(at).wait_send()
    for at in range(3):
        x_copy(at).wait_send()


def neighbour_sums(features, slots, counts, tiles):
    hbm = pl.BlockSpec(memory_space=pl.ANY)
    return pl.pallas_call(
        sum_kernel,
        in_specs=[hbm, hbm, hbm, pl.BlockSpec(memory_space=pltpu.SMEM)],
        out_specs=pl.BlockSpec(memory_space=pltpu.VMEM),
        scratch_shapes=[
            pltpu.VMEM((48, 16384), BF),
            pltpu.VMEM((128, 192, 128), BF),
            pltpu.VMEM((8, 16, 1024), jnp.int32),
            pltpu.VMEM((8, 8, 1024), jnp.int32),
            pltpu.VMEM((128, 128), jnp.int32),
            pltpu.VMEM((128, 128), jnp.int32),
            pltpu.VMEM((64, 8, 128, 256), BF),
            pltpu.VMEM((4, 192, 1024), F32),
            pltpu.VMEM((4, 192, 1024), F32),
            pltpu.VMEM((3, 192, 1024), BF),
            pltpu.VMEM((3, 192, 1024), BF),
            pltpu.VMEM((192, 1024), F32),
            pltpu.SemaphoreType.DMA((3,)),
            pltpu.SemaphoreType.DMA((2, 6)),
            pltpu.SemaphoreType.DMA((2, 4)),
            pltpu.SemaphoreType.DMA((2, 3)),
        ],
        out_shape=jax.ShapeDtypeStruct((192, 1024), BF),
        compiler_params=pltpu.CompilerParams(vmem_limit_bytes=60 << 20, collective_id=0, has_side_effects=True),
    )(features, slots, counts, tiles)


def per_device(features, sampled_slots, block_index, counts, weight, cotangent):
    feat, batch = lax.axis_index("feat"), lax.axis_index("batch")
    z, y, x, core = feat // 4, feat % 4, batch // 2, batch % 2

    def around_z(array):
        return [array] + [along_z(array, -step) for step in (1, 2, 3)]

    aggregate = neighbour_sums(features, sampled_slots, counts, block_index.reshape(8, 512))
    weights = jnp.concatenate(around_z(weight), 0)

    def rows_of(step):
        return lax.dynamic_slice(aggregate, (0, (y + step) % 4 * 256), (192, 256))

    rows = [rows_of(step) for step in range(4)]
    parts = [jnp.einsum("dr,dh->rh", block, weights, preferred_element_type=F32) for block in rows]
    preact = parts[0]
    for step in (1, 2, 3):
        preact = preact + along_y(parts[step].astype(BF), step).astype(F32)
    sigmoid_val = jax.nn.sigmoid(preact)
    hidden = (preact * sigmoid_val).astype(BF)
    pre_grad = (cotangent.astype(F32) * sigmoid_val * (1.0 + preact * (1.0 - sigmoid_val))).astype(BF)
    grad = jnp.dot(rows[0], pre_grad, preferred_element_type=F32)
    for step in (1, 2, 3):
        grad = grad + jnp.dot(rows[step], along_y(pre_grad, -step), preferred_element_type=F32)
    grad = grad.reshape(4, 48, 1024)
    weight_grad = grad[0]
    for step in (1, 2, 3):
        weight_grad = weight_grad + along_z(grad[step], step)
    for bit in (1, 2, 4):
        weight_grad = weight_grad + flip(weight_grad, bit)
    return hidden, weight_grad


def solution(mesh):
    placed = (
        P("feat", "batch"),
        P(None, "batch", None, None),
        P(None, "batch", None, None),
        P(),
        P("feat", None),
        P(("feat", "batch"), None),
    )
    return jax.shard_map(
        per_device,
        mesh=mesh,
        in_specs=placed,
        out_specs=(P(("feat", "batch"), None), P("feat", None)),
        check_vma=False,
    )
```

time: 243 us -> 185 us (0.76)
  waiting for transfers between devices: 146 us -> 64.3 us
  Pallas kernels: 46.3 us -> 89.3 us
  starting transfers between devices: 30.8 us -> 20.7 us
  local copies, waits for them, and re-layouts: 9.17 us -> 1.74 us
  other arithmetic: 3.9 us -> 0.8 us
    ppermute x22 -> x15, waiting for transfers between devices: 146 us -> 64.3 us  [shift(): return lax.ppermute(array, axis, [(at, move(at)) for at in range(size)])]
    pallas_call x1, Pallas kernels: 46.3 us -> 89.3 us  [neighbour_sums(): pl.pallas_call(sum_kernel, in_specs=[hbm, hbm, hbm, pl.BlockSpec(memory_s...]
    ppermute x22 -> x15, starting transfers between devices: 30.8 us -> 20.7 us  [shift(): return lax.ppermute(array, axis, [(at, move(at)) for at in range(size)])]
    unnamed x16 -> x10, local copies, waits for them, and re-layouts: 6.28 us -> 0.97 us
  transfers between devices with their start and end apart: 22 -> 15, of which waited for: 16 -> 11; matrix products, arithmetic and copies ran while one was open for 3% -> 2% of each run, Pallas kernels for 0% -> 48%
where the time goes in v2:
time: 185 us; the launch traced here: 184 us
  Pallas kernels  89.3 us (48%)
  waiting for transfers between devices  64.3 us (35%)
  starting transfers between devices  20.7 us (11%)
  matrix products  6.69 us (4%)
    pallas_call x1, Pallas kernels, neighbour_sums(): pl.pallas_call(sum_kernel, in_specs=[hbm, hbm, hbm, pl.BlockSpec(memory_s...  89.3 us
    ppermute x15, waiting for transfers between devices, shift(): return lax.ppermute(array, axis, [(at, move(at)) for at in range(size)])  64.3 us
    ppermute x15, starting transfers between devices, shift(): return lax.ppermute(array, axis, [(at, move(at)) for at in range(size)])  20.7 us
    dot_general x4, matrix products, per_device(): jnp.einsum('dr,dh->rh', block, weights, preferred_element_type=F32)  5.6 us
  transfers between devices with their start and end apart: 15, of which 11 were waited for; matrix products, arithmetic and copies ran while one was open for 2% of the time, Pallas kernels for 48%

profile of v2, /device:TPU:1, one launch (start us, length us, event | category | flops | bytes accessed | tf_op | source)
XLA Modules:
  0.0 184.3 jit_solution(3252892232944659352)
XLA Ops:
  0.6 4.7 %collective-permute-start = (bf16[48,1024]{1,0:T(8,128)(2,1)}, bf16[48,1024]{1,0:T(8,128)(2,1)S(1)}, u32[]{:S(2)}, u32[]{:S(2)}) collective-permute-start(bf16[48,1024]{1,0:T(8,128)(2,1)} %param.10), channel_id=1, source_target_pairs={{0,96},{8,104},{16,112},{24,120},{32,0},{40,8},{48,16},{56,24},{64... | collective-permute-start | bytes 294920 | tf_op jit(solution)/shard_map/ppermute | solution.py:15
  5.3 0.0 collective-permute-start.1
  5.3 0.7 collective-permute-start.2
  6.0 0.9 copy.9
  6.9 0.7 reshape.16.tiles
  7.6 0.0 copy-start.1
  7.6 89.3 %shard_map.77 = bf16[192,1024]{1,0:T(8,128)(2,1)} custom-call(bf16[48,16384]{1,0:T(8,128)(2,1)} %features.1, s32[8,1,16,4096]{3,2,1,0:T(8,128)} %slots.1, s32[8,8,4096]{2,1,0:T(8,128)} %counts.1, s32[8,512]{1,0:T(8,128)} %reshape.16.tiles), custom_call_target="tpu_custom_call" | custom-call | tf_op jit(solution)/shard_map/pallas_call | solution.py:230
  97.0 0.0 copy-done.1
  97.0 0.0 copy-start
  97.0 0.0 copy-start.2
  97.0 0.0 collective-permute-done
  97.0 0.0 collective-permute-done.1
  97.1 0.0 collective-permute-done.2
  97.1 1.3 convolution_convert_fusion.2
  98.4 1.4 collective-permute-start.3
  99.7 1.2 convolution_convert_fusion.1
  100.9 2.7 %collective-permute-start.4 = (bf16[256,1024]{1,0:T(8,128)(2,1)S(1)}, bf16[256,1024]{1,0:T(8,128)(2,1)}, u32[]{:S(2)}, u32[]{:S(2)}) collective-permute-start(bf16[256,1024]{1,0:T(8,128)(2,1)S(1)} %convolution_convert_fusion.1), channel_id=1, source_target_pairs={{0,16},{8,24},{16,0},{24,8},{32,48},{40,56},{48,32},{56,40},{64,80... | collective-permute-start | bytes 1572872 | tf_op jit(solution)/shard_map/ppermute | solution.py:15
  103.7 0.0 copy-done
  103.7 0.3 convolution_convert_fusion
  104.0 1.1 collective-permute-start.5
  105.1 7.7 %collective-permute-done.3 = bf16[256,1024]{1,0:T(8,128)(2,1)S(1)} collective-permute-done((bf16[256,1024]{1,0:T(8,128)(2,1)S(1)}, bf16[256,1024]{1,0:T(8,128)(2,1)S(1)}, u32[]{:S(2)}, u32[]{:S(2)}) %collective-permute-start.3) | collective-permute-done | bytes 524320 | tf_op jit(solution)/shard_map/ppermute | solution.py:15
  112.8 12.4 %collective-permute-done.4 = bf16[256,1024]{1,0:T(8,128)(2,1)} collective-permute-done((bf16[256,1024]{1,0:T(8,128)(2,1)S(1)}, bf16[256,1024]{1,0:T(8,128)(2,1)}, u32[]{:S(2)}, u32[]{:S(2)}) %collective-permute-start.4) | collective-permute-done | bytes 524320 | tf_op jit(solution)/shard_map/ppermute | solution.py:15
  125.2 0.5 collective-permute-done.5
  125.8 0.0 copy-done.2
  125.8 2.8 %multiply_convert_fusion = (bf16[256,1024]{1,0:T(8,128)(2,1)S(1)}, bf16[256,1024]{1,0:T(8,128)(2,1)}) fusion(bf16[256,1024]{1,0:T(8,128)(2,1)S(1)} %copy-done.2, bf16[256,1024]{1,0:T(8,128)(2,1)} %collective-permute-done.5, bf16[256,1024]{1,0:T(8,128)(2,1)} %collective-permute-done.4, bf16[256,1024]{1,0:T(8,128)(2,1)S(1)} %collective-permute-done.3, ...), kind=kOutput, calls=%fused_computation.9 | convolution fusion | flops 105381888 | bytes 3637252 | tf_op jit(solution)/shard_map/dr,dh->rh/dot_general | solution.py:271
  128.6 2.5 %collective-permute-start.8 = (bf16[256,1024]{1,0:T(8,128)(2,1)S(1)}, bf16[256,1024]{1,0:T(8,128)(2,1)S(1)}, u32[]{:S(2)}, u32[]{:S(2)}) collective-permute-start(bf16[256,1024]{1,0:T(8,128)(2,1)S(1)} %get-tuple-element.2), channel_id=1, source_target_pairs={{0,8},{8,16},{16,24},{24,0},{32,40},{40,48},{48,56},{56,32},{64,72... | collective-permute-start | bytes 1572872 | tf_op jit(solution)/shard_map/ppermute | solution.py:15
  131.0 0.9 collective-permute-start.6
  132.0 1.2 collective-permute-start.7
  133.2 0.3 fusion.12
  133.4 9.7 %collective-permute-done.8 = bf16[256,1024]{1,0:T(8,128)(2,1)S(1)} collective-permute-done((bf16[256,1024]{1,0:T(8,128)(2,1)S(1)}, bf16[256,1024]{1,0:T(8,128)(2,1)S(1)}, u32[]{:S(2)}, u32[]{:S(2)}) %collective-permute-start.8) | collective-permute-done | bytes 524320 | tf_op jit(solution)/shard_map/ppermute | solution.py:15
  143.1 0.3 fusion.5
  143.4 0.0 collective-permute-done.6
  143.4 0.3 convolution_add_fusion.2
  143.7 12.2 %collective-permute-done.7 = bf16[256,1024]{1,0:T(8,128)(2,1)S(1)} collective-permute-done((bf16[256,1024]{1,0:T(8,128)(2,1)S(1)}, bf16[256,1024]{1,0:T(8,128)(2,1)S(1)}, u32[]{:S(2)}, u32[]{:S(2)}) %collective-permute-start.7) | collective-permute-done | bytes 524320 | tf_op jit(solution)/shard_map/ppermute | solution.py:15
  155.9 0.3 fusion.2
  156.3 1.6 collective-permute-start.10
  157.8 0.8 collective-permute-start.11
  158.6 0.7 collective-permute-start.9
  159.3 3.6 %collective-permute-done.10 = f32[48,1024]{1,0:T(8,128)S(1)} collective-permute-done((f32[48,1024]{1,0:T(8,128)S(1)}, f32[48,1024]{1,0:T(8,128)S(1)}, u32[]{:S(2)}, u32[]{:S(2)}) %collective-permute-start.10) | collective-permute-done | bytes 196640 | tf_op jit(solution)/shard_map/ppermute | solution.py:15
  162.9 2.5 %collective-permute-done.11 = f32[48,1024]{1,0:T(8,128)S(1)} collective-permute-done((f32[48,1024]{1,0:T(8,128)S(1)}, f32[48,1024]{1,0:T(8,128)S(1)}, u32[]{:S(2)}, u32[]{:S(2)}) %collective-permute-start.11) | collective-permute-done | bytes 196640 | tf_op jit(solution)/shard_map/ppermute | solution.py:15
  165.4 2.5 %collective-permute-done.9 = f32[48,1024]{1,0:T(8,128)S(1)} collective-permute-done((f32[48,1024]{1,0:T(8,128)S(1)}, f32[48,1024]{1,0:T(8,128)S(1)}, u32[]{:S(2)}, u32[]{:S(2)}) %collective-permute-start.9) | collective-permute-done | bytes 196640 | tf_op jit(solution)/shard_map/ppermute | solution.py:15
  167.9 0.1 fusion.4
  168.0 1.5 collective-permute-start.12
  169.5 1.1 collective-permute-done.12
  170.6 0.1 collective-permute-start.13
  170.7 6.1 %collective-permute-done.13 = f32[48,1024]{1,0:T(8,128)S(1)} collective-permute-done((f32[48,1024]{1,0:T(8,128)S(1)}, f32[48,1024]{1,0:T(8,128)S(1)}, u32[]{:S(2)}, u32[]{:S(2)}) %collective-permute-start.13) | collective-permute-done | bytes 196640 | tf_op jit(solution)/shard_map/ppermute | solution.py:15
  176.8 0.8 collective-permute-start.14
  177.7 5.9 %collective-permute-done.14 = f32[48,1024]{1,0:T(8,128)S(1)} collective-permute-done((f32[48,1024]{1,0:T(8,128)S(1)}, f32[48,1024]{1,0:T(8,128)S(1)}, u32[]{:S(2)}, u32[]{:S(2)}) %collective-permute-start.14) | collective-permute-done | bytes 196640 | tf_op jit(solution)/shard_map/ppermute | solution.py:15
  183.6 0.7 add.104
  (7 shorter events, 0.1 us)
Async XLA Ops:
  0.6 96.4 %collective-permute-start = (bf16[48,1024]{1,0:T(8,128)(2,1)}, bf16[48,1024]{1,0:T(8,128)(2,1)S(1)}, u32[]{:S(2)}, u32[]{:S(2)}) collective-permute-start(bf16[48,1024]{1,0:T(8,128)(2,1)} %param.10), channel_id=1, source_target_pairs={{0,96},{8,104},{16,112},{24,120},{32,0},{40,8},{48,16},{56,24},{64... | collective-permute-start | bytes 294920 | tf_op jit(solution)/shard_map/ppermute | solution.py:15
  5.3 91.7 %collective-permute-start.1 = (bf16[48,1024]{1,0:T(8,128)(2,1)}, bf16[48,1024]{1,0:T(8,128)(2,1)S(1)}, u32[]{:S(2)}, u32[]{:S(2)}) collective-permute-start(bf16[48,1024]{1,0:T(8,128)(2,1)} %param.10), channel_id=1, source_target_pairs={{0,64},{8,72},{16,80},{24,88},{32,96},{40,104},{48,112},{56,120},{... | collective-permute-start | bytes 294920 | tf_op jit(solution)/shard_map/ppermute | solution.py:15
  5.3 91.8 %collective-permute-start.2 = (bf16[48,1024]{1,0:T(8,128)(2,1)}, bf16[48,1024]{1,0:T(8,128)(2,1)S(1)}, u32[]{:S(2)}, u32[]{:S(2)}) collective-permute-start(bf16[48,1024]{1,0:T(8,128)(2,1)} %param.10), channel_id=1, source_target_pairs={{0,32},{8,40},{16,48},{24,56},{32,64},{40,72},{48,80},{56,88},{64,... | collective-permute-start | bytes 294920 | tf_op jit(solution)/shard_map/ppermute | solution.py:15
  7.6 89.3 %copy-start.1 = (bf16[48,1024]{1,0:T(8,128)(2,1)S(1)}, bf16[48,1024]{1,0:T(8,128)(2,1)}, u32[]{:S(2)}) copy-start(bf16[48,1024]{1,0:T(8,128)(2,1)} %param.10) | copy-start | bytes 294916
  97.0 6.7 %copy-start = (bf16[192,1024]{1,0:T(8,128)(2,1)S(1)}, bf16[192,1024]{1,0:T(8,128)(2,1)}, u32[]{:S(2)}) copy-start(bf16[192,1024]{1,0:T(8,128)(2,1)} %shard_map.77) | copy-start | bytes 1179652
  97.0 28.8 %copy-start.2 = (bf16[256,1024]{1,0:T(8,128)(2,1)S(1)}, bf16[256,1024]{1,0:T(8,128)(2,1)}, u32[]{:S(2)}) copy-start(bf16[256,1024]{1,0:T(8,128)(2,1)} %param.11) | copy-start | bytes 1572868
  98.4 14.4 %collective-permute-start.3 = (bf16[256,1024]{1,0:T(8,128)(2,1)S(1)}, bf16[256,1024]{1,0:T(8,128)(2,1)S(1)}, u32[]{:S(2)}, u32[]{:S(2)}) collective-permute-start(bf16[256,1024]{1,0:T(8,128)(2,1)S(1)} %convolution_convert_fusion.2), channel_id=1, source_target_pairs={{0,8},{8,16},{16,24},{24,0},{32,40},{40,48},{48,56},{56,32},{64,72... | collective-permute-start | bytes 1572872 | tf_op jit(solution)/shard_map/ppermute | solution.py:15
  100.9 24.3 %collective-permute-start.4 = (bf16[256,1024]{1,0:T(8,128)(2,1)S(1)}, bf16[256,1024]{1,0:T(8,128)(2,1)}, u32[]{:S(2)}, u32[]{:S(2)}) collective-permute-start(bf16[256,1024]{1,0:T(8,128)(2,1)S(1)} %convolution_convert_fusion.1), channel_id=1, source_target_pairs={{0,16},{8,24},{16,0},{24,8},{32,48},{40,56},{48,32},{56,40},{64,80... | collective-permute-start | bytes 1572872 | tf_op jit(solution)/shard_map/ppermute | solution.py:15
  104.0 21.8 %collective-permute-start.5 = (bf16[256,1024]{1,0:T(8,128)(2,1)S(1)}, bf16[256,1024]{1,0:T(8,128)(2,1)}, u32[]{:S(2)}, u32[]{:S(2)}) collective-permute-start(bf16[256,1024]{1,0:T(8,128)(2,1)S(1)} %convolution_convert_fusion), channel_id=1, source_target_pairs={{0,24},{8,0},{16,8},{24,16},{32,56},{40,32},{48,40},{56,48},{64,88... | collective-permute-start | bytes 1572872 | tf_op jit(solution)/shard_map/ppermute | solution.py:15
  128.6 14.6 %collective-permute-start.8 = (bf16[256,1024]{1,0:T(8,128)(2,1)S(1)}, bf16[256,1024]{1,0:T(8,128)(2,1)S(1)}, u32[]{:S(2)}, u32[]{:S(2)}) collective-permute-start(bf16[256,1024]{1,0:T(8,128)(2,1)S(1)} %get-tuple-element.2), channel_id=1, source_target_pairs={{0,8},{8,16},{16,24},{24,0},{32,40},{40,48},{48,56},{56,32},{64,72... | collective-permute-start | bytes 1572872 | tf_op jit(solution)/shard_map/ppermute | solution.py:15
  131.0 12.4 %collective-permute-start.6 = (bf16[256,1024]{1,0:T(8,128)(2,1)S(1)}, bf16[256,1024]{1,0:T(8,128)(2,1)S(1)}, u32[]{:S(2)}, u32[]{:S(2)}) collective-permute-start(bf16[256,1024]{1,0:T(8,128)(2,1)S(1)} %get-tuple-element.2), channel_id=1, source_target_pairs={{0,24},{8,0},{16,8},{24,16},{32,56},{40,32},{48,40},{56,48},{64,88... | collective-permute-start | bytes 1572872 | tf_op jit(solution)/shard_map/ppermute | solution.py:15
  132.0 23.9 %collective-permute-start.7 = (bf16[256,1024]{1,0:T(8,128)(2,1)S(1)}, bf16[256,1024]{1,0:T(8,128)(2,1)S(1)}, u32[]{:S(2)}, u32[]{:S(2)}) collective-permute-start(bf16[256,1024]{1,0:T(8,128)(2,1)S(1)} %get-tuple-element.2), channel_id=1, source_target_pairs={{0,16},{8,24},{16,0},{24,8},{32,48},{40,56},{48,32},{56,40},{64,80... | collective-permute-start | bytes 1572872 | tf_op jit(solution)/shard_map/ppermute | solution.py:15
  156.3 6.6 %collective-permute-start.10 = (f32[48,1024]{1,0:T(8,128)S(1)}, f32[48,1024]{1,0:T(8,128)S(1)}, u32[]{:S(2)}, u32[]{:S(2)}) collective-permute-start(f32[48,1024]{1,0:T(8,128)S(1)} %get-tuple-element.6), channel_id=1, source_target_pairs={{0,64},{8,72},{16,80},{24,88},{32,96},{40,104},{48,112},{56,120},{... | collective-permute-start | bytes 589832 | tf_op jit(solution)/shard_map/ppermute | solution.py:15
  157.8 7.6 %collective-permute-start.11 = (f32[48,1024]{1,0:T(8,128)S(1)}, f32[48,1024]{1,0:T(8,128)S(1)}, u32[]{:S(2)}, u32[]{:S(2)}) collective-permute-start(f32[48,1024]{1,0:T(8,128)S(1)} %get-tuple-element.5), channel_id=1, source_target_pairs={{0,96},{8,104},{16,112},{24,120},{32,0},{40,8},{48,16},{56,24},{64... | collective-permute-start | bytes 589832 | tf_op jit(solution)/shard_map/ppermute | solution.py:15
  158.6 9.3 %collective-permute-start.9 = (f32[48,1024]{1,0:T(8,128)S(1)}, f32[48,1024]{1,0:T(8,128)S(1)}, u32[]{:S(2)}, u32[]{:S(2)}) collective-permute-start(f32[48,1024]{1,0:T(8,128)S(1)} %get-tuple-element.4), channel_id=1, source_target_pairs={{0,32},{8,40},{16,48},{24,56},{32,64},{40,72},{48,80},{56,88},{64,... | collective-permute-start | bytes 589832 | tf_op jit(solution)/shard_map/ppermute | solution.py:15
  168.0 2.6 %collective-permute-start.12 = (f32[48,1024]{1,0:T(8,128)S(1)}, f32[48,1024]{1,0:T(8,128)S(1)}, u32[]{:S(2)}, u32[]{:S(2)}) collective-permute-start(f32[48,1024]{1,0:T(8,128)S(1)} %fusion.4), channel_id=1, source_target_pairs={{0,1},{1,0},{2,3},{3,2},{4,5},{5,4},{6,7},{7,6},{8,9},{9,8},{10,11... | collective-permute-start | bytes 589832 | tf_op jit(solution)/shard_map/ppermute | solution.py:15
  170.6 6.2 %collective-permute-start.13 = (f32[48,1024]{1,0:T(8,128)S(1)}, f32[48,1024]{1,0:T(8,128)S(1)}, u32[]{:S(2)}, u32[]{:S(2)}) collective-permute-start(f32[48,1024]{1,0:T(8,128)S(1)} %add.102), channel_id=1, source_target_pairs={{0,2},{1,3},{2,0},{3,1},{4,6},{5,7},{6,4},{7,5},{8,10},{9,11},{10,... | collective-permute-start | bytes 589832 | tf_op jit(solution)/shard_map/ppermute | solution.py:15
  176.8 6.8 %collective-permute-start.14 = (f32[48,1024]{1,0:T(8,128)S(1)}, f32[48,1024]{1,0:T(8,128)S(1)}, u32[]{:S(2)}, u32[]{:S(2)}) collective-permute-start(f32[48,1024]{1,0:T(8,128)S(1)} %add.103), channel_id=1, source_target_pairs={{0,4},{1,5},{2,6},{3,7},{4,0},{5,1},{6,2},{7,3},{8,12},{9,13},{10,... | collective-permute-start | bytes 589832 | tf_op jit(solution)/shard_map/ppermute | solution.py:15

commit v3 on v2

v3 whole, which is shorter than its diff:
```python
import jax
import jax.numpy as jnp
from jax import lax
from jax.experimental import pallas as pl
from jax.experimental.pallas import tpu as pltpu
from jax.sharding import PartitionSpec as P

BF = jnp.bfloat16
F32 = jnp.float32
NT = (((1,), (1,)), ((), ()))


def edge_codes(slots, used):
    slot_row = lax.broadcasted_iota(jnp.int32, slots.shape, 0) & 15
    lane = lax.broadcasted_iota(jnp.int32, slots.shape, 1)
    height = slots.shape[0]
    value = jnp.where(slot_row < used, slots, -1)
    for bit in range(4):
        rows, lanes = 1 << bit, 8 << bit
        row_bit = (slot_row >> bit) & 1
        lane_bit = (lane >> (bit + 3)) & 1
        later = pltpu.roll(pltpu.roll(value, height - rows, 0), lanes, 1)
        earlier = pltpu.roll(pltpu.roll(value, rows, 0), 128 - lanes, 1)
        value = jnp.where(row_bit < lane_bit, later, jnp.where(row_bit > lane_bit, earlier, value))
    return (value >> 7) * 8 + (lane & 7), value & 127


def onehot(code):
    rows = lax.broadcasted_iota(jnp.int32, (128, 128), 0).astype(BF)
    match = jnp.broadcast_to(code.astype(BF), (128, 128)) == rows
    return jnp.where(match, BF(1), BF(0))


def build(adjacency, pairs_at, block, tile_codes, node_codes):
    blank = jnp.zeros((128, 128), BF)
    for pair in range(8):
        row = block * 16 + 2 * pair
        tile_a, tile_b = onehot(tile_codes[pl.ds(row, 1)]), onehot(tile_codes[pl.ds(row + 1, 1)])
        node_a, node_b = onehot(node_codes[pl.ds(row, 1)]), onehot(node_codes[pl.ds(row + 1, 1)])
        both = lax.dot_general(
            jnp.concatenate([tile_a, tile_b], 1),
            jnp.concatenate([jnp.concatenate([node_a, blank], 1), jnp.concatenate([blank, node_b], 1)], 0),
            NT,
            preferred_element_type=F32,
        )
        rows = jnp.concatenate([both[:, :128].reshape(16, 8, 128), both[:, 128:].reshape(16, 8, 128)], 1).astype(BF)
        for tile in range(16):
            adjacency[pairs_at, tile // 2, pair * 16:pair * 16 + 16, tile % 2 * 128:tile % 2 * 128 + 128] = rows[tile]


def remote(src, dst, sems, at, target):
    return pltpu.make_async_remote_copy(
        src_ref=src, dst_ref=dst, send_sem=sems.at[0, at], recv_sem=sems.at[1, at],
        device_id=target, device_id_type=pl.DeviceIdType.MESH,
    )


def layer_kernel(
    features, slots, counts, tiles, weight, cotangent, hidden, weight_grad,
    raw, near, far, slot_rows, used, tile_codes, node_codes, adjacency,
    core_near_out, core_near_in, core_far_out, core_far_in,
    x_near_out, x_near_in, x_far_out, x_far_in, own_near, own_far,
    weights, aggregate, rows, rows_t, cot, grad_out, grad_in, grad_y_out, grad_y_in, grad_own,
    grad_z_out, grad_z_in, grad_x_out, grad_x_in, pieces,
    load_sems, z_sems, w_sems, core_sems, x_sems, y_sems, grad_core_sems, grad_y_sems, grad_z_sems, grad_x_sems, piece_sems,
):
    feat, batch = lax.axis_index("feat"), lax.axis_index("batch")
    z, y, x, core = feat // 4, feat % 4, batch // 2, batch % 2
    piece = core * 4 + x

    def z_at(step):
        return (lax.rem(z + step, 4) * 4 + y, batch)

    def y_at(step):
        return (z * 4 + lax.rem(y + step, 4), batch)

    def x_at(step, side=0):
        return (feat, lax.rem(x + step, 4) * 2 + lax.rem(core + side, 2))

    partner = x_at(0, 1)
    others = [x_at(step, side) for step in range(4) for side in range(2)][1:]
    barrier = pltpu.get_barrier_semaphore()
    greeted = [z_at(1), z_at(2), z_at(3), y_at(1), y_at(2), y_at(3)] + others
    for device in greeted:
        pl.semaphore_signal(barrier, inc=1, device_id=device, device_id_type=pl.DeviceIdType.MESH)
    own_columns = pl.ds(pl.multiple_of(z * 1024, 1024), 1024)
    piece_columns = pl.ds(pl.multiple_of(piece * 128, 128), 128)
    loads = [
        pltpu.make_async_copy(features, raw, load_sems.at[0]),
        pltpu.make_async_copy(weight.at[:, piece_columns], weights.at[piece, pl.ds(0, 48)], load_sems.at[1]),
        pltpu.make_async_copy(slots.at[:, 0, :, own_columns], slot_rows, load_sems.at[2]),
        pltpu.make_async_copy(counts.at[:, :, own_columns], used, load_sems.at[3]),
        pltpu.make_async_copy(cotangent, cot, load_sems.at[4]),
    ]
    for load in loads:
        load.start()
    loads[0].wait()
    for tile in range(128):
        near[tile, 0:48, :] = raw[:, tile * 128:tile * 128 + 128]
    loads[1].wait()
    pl.semaphore_wait(barrier, len(greeted))

    low, high = pl.ds(0, 64), pl.ds(64, 64)

    def shard(at, part):
        return near.at[part, pl.ds(48 * at, 48), :]

    ring = [
        remote(shard(0, low), shard(2, low), z_sems, 0, z_at(1)),
        remote(shard(0, high), shard(1, high), z_sems, 1, z_at(3)),
        remote(shard(0, high), shard(2, high), z_sems, 2, z_at(1)),
        remote(shard(0, low), shard(1, low), z_sems, 3, z_at(3)),
        remote(shard(2, low), far.at[low], z_sems, 4, z_at(1)),
        remote(shard(1, high), far.at[high], z_sems, 5, z_at(3)),
    ]

    mine = weights.at[piece]
    w_first = mine.at[pl.ds(0, 48)]
    w_z = [
        remote(w_first, mine.at[pl.ds(48 * {1: 2, 2: 3, 3: 1}[step], 48)], w_sems, step - 1, z_at(step))
        for step in (1, 2, 3)
    ]
    w_y = [
        remote(mine.at[pl.ds(0, 192)], mine.at[pl.ds(192 * (4 - step), 192)], w_sems, 2 + step, y_at(step))
        for step in (1, 2, 3)
    ]
    w_all = [
        remote(mine, mine, w_sems, 6 + at, device) for at, device in enumerate(others)
    ]
    for copy in w_z:
        copy.start()
    ring[0].start()
    ring[1].start()
    loads[2].wait()
    loads[3].wait()

    def group_at(step):
        return lax.rem(x + 3 - step % 4, 4) * 2 + lax.rem(core + 1 - step // 4, 2)

    def build_group(step, unused):
        group = group_at(step)
        group_used = used[group, pl.ds(batch, 1), :]
        tile_code, node_code = edge_codes(
            jnp.concatenate([slot_rows[group, :, b * 128:b * 128 + 128] for b in range(8)], 0),
            jnp.concatenate([jnp.broadcast_to(group_used[:, b * 128:b * 128 + 128], (16, 128)) for b in range(8)], 0),
        )
        tile_codes[...] = tile_code
        node_codes[...] = node_code

        def some(turn, unused):
            for at in range(4):
                build(adjacency, step * 8 + turn * 4 + at, turn * 4 + at, tile_codes, node_codes)
            return 0

        return lax.fori_loop(0, 2, some, 0)

    lax.fori_loop(0, 2, build_group, 0)
    for copy in w_z:
        copy.wait_recv()
    for copy in w_y:
        copy.start()
    lax.fori_loop(2, 4, build_group, 0)
    ring[2].start()
    ring[3].start()
    for copy in w_y:
        copy.wait_recv()
    for copy in w_all:
        copy.start()
    lax.fori_loop(4, 8, build_group, 0)
    ring[0].wait_recv()
    ring[1].wait_recv()
    ring[4].start()
    ring[5].start()
    ring[2].wait_recv()
    ring[3].wait_recv()

    def products(feats, step, put):
        group = group_at(step)

        def one(block):
            total = jnp.zeros((feats.shape[1], 128), F32)
            for pair in range(8):
                entry = (z * 8 + block) * 16 + pair * 2
                halves = [feats[tiles[group, entry + half]] for half in range(2)]
                total += lax.dot_general(
                    jnp.concatenate(halves, 1), adjacency[step * 8 + block, pair], NT, preferred_element_type=F32
                )
            put(pl.ds(pl.multiple_of(block * 128, 128), 128), total)

        def some(turn, unused):
            for at in range(4):
                one(turn * 4 + at)
            return 0

        lax.fori_loop(0, 2, some, 0)

    def exchange(feats, core_out, core_in, x_out, x_in, own, core_base, x_base):
        def core_copy(at):
            return remote(core_out.at[at], core_in.at[at], core_sems, core_base + at, partner)

        def x_copy(at):
            return remote(x_out.at[at], x_in.at[at], x_sems, x_base + at, x_at(3 - at))

        def for_partner(step, unused):
            def put(columns, total):
                core_out[step, :, columns] = total

            products(feats, step, put)
            core_copy(step).start()
            return 0

        def for_x(at, unused):
            core_copy(at).wait_recv()

            def put(columns, total):
                x_out[at, :, columns] = (total + core_in[at, :, columns]).astype(BF)

            products(feats, at + 4, put)
            x_copy(at).start()
            return 0

        def put_own(columns, total):
            own[:, columns] = total + core_in[3, :, columns]

        lax.fori_loop(0, 4, for_partner, 0)
        lax.fori_loop(0, 3, for_x, 0)
        core_copy(3).wait_recv()
        products(feats, 7, put_own)
        return [core_copy(at) for at in range(4)], [x_copy(at) for at in range(3)]

    totals = jnp.sum(used[batch], axis=0, keepdims=True).astype(F32)

    def average(x_copies, own, x_in, first):
        for copy in x_copies:
            copy.wait_recv()
        height = own.shape[0]
        for chunk in range(4):
            columns = slice(chunk * 256, chunk * 256 + 256)
            summed = own[:, columns]
            for at in range(3):
                summed = summed + x_in[at, :, columns].astype(F32)
            aggregate[chunk, first:first + height, :] = (summed / totals[:, columns]).astype(BF)

    near_core, near_x = exchange(near, core_near_out, core_near_in, x_near_out, x_near_in, own_near, 0, 0)
    ring[4].wait_recv()
    ring[5].wait_recv()
    far_core, far_x = exchange(far, core_far_out, core_far_in, x_far_out, x_far_in, own_far, 4, 3)
    average(near_x, own_near, x_near_in, 0)
    average(far_x, own_far, x_far_in, 144)

    y_copies = [
        remote(aggregate.at[lax.rem(y + step, 4)], rows.at[4 - step], y_sems, step - 1, y_at(step)) for step in (1, 2, 3)
    ]
    for copy in y_copies:
        copy.start()
    rows[0] = aggregate[y]
    for copy in w_all:
        copy.wait_recv()
    loads[4].wait()
    for copy in y_copies:
        copy.wait_recv()
    rows_t[...] = rows[...].reshape(768, 256).T

    def layer(tile):
        columns = pl.ds(pl.multiple_of(tile * 256, 256), 256)
        preact = jnp.dot(
            rows_t[...], jnp.concatenate([weights[tile * 2], weights[tile * 2 + 1]], 1), preferred_element_type=F32
        )
        sigmoid_val = jax.nn.sigmoid(preact)
        hidden[:, columns] = (preact * sigmoid_val).astype(BF)
        pre_grad = cot[:, columns].astype(F32) * sigmoid_val * (1.0 + preact * (1.0 - sigmoid_val))
        return jnp.dot(rows[...].reshape(768, 256), pre_grad.astype(BF), preferred_element_type=F32)

    grad_core = [remote(grad_out.at[at], grad_in.at[at], grad_core_sems, at, partner) for at in range(2)]
    for at in range(2):
        grad_out[at] = layer((1 - core) * 2 + at)
        grad_core[at].start()
    grad_y = []
    for at in range(2):
        grad = layer(core * 2 + at)
        grad_core[at].wait_recv()
        grad = grad + grad_in[at]
        grad_own[at] = grad[0:192]
        for step in (1, 2, 3):
            slot = at * 3 + step - 1
            grad_y_out[slot] = grad[step * 192:step * 192 + 192].astype(BF)
            grad_y.append(remote(grad_y_out.at[slot], grad_y_in.at[slot], grad_y_sems, slot, y_at(step)))
            grad_y[slot].start()
    grad_z = []
    for at in range(2):
        grad = grad_own[at]
        for step in (1, 2, 3):
            grad_y[at * 3 + step - 1].wait_recv()
            grad = grad + grad_y_in[at * 3 + step - 1].astype(F32)
        grad_own[at] = grad
        for shard_at, step in ((1, 1), (2, 3), (3, 2)):
            slot = at * 3 + shard_at - 1
            grad_z_out[slot] = grad[shard_at * 48:shard_at * 48 + 48].astype(BF)
            grad_z.append(remote(grad_z_out.at[slot], grad_z_in.at[slot], grad_z_sems, slot, z_at(step)))
            grad_z[slot].start()
    for at in range(2):
        grad = grad_own[at, 0:48]
        for slot in range(at * 3, at * 3 + 3):
            grad_z[slot].wait_recv()
            grad = grad + grad_z_in[slot].astype(F32)
        grad_x_out[at * 2] = grad[:, :128]
        grad_x_out[at * 2 + 1] = grad[:, 128:]
    grad_x = [
        remote(grad_x_out.at[lax.rem(x + step, 4)], grad_x_in.at[step - 1], grad_x_sems, step - 1, x_at(step))
        for step in (1, 2, 3)
    ]
    for copy in grad_x:
        copy.start()
    grad = grad_x_out[x]
    for step in range(3):
        grad_x[step].wait_recv()
        grad = grad + grad_x_in[step]
    pieces[piece] = grad
    spread = [remote(pieces.at[piece], pieces.at[piece], piece_sems, at, device) for at, device in enumerate(others)]
    for copy in spread:
        copy.start()
    for copy in spread:
        copy.wait_recv()
    for at in range(8):
        weight_grad[:, at * 128:at * 128 + 128] = pieces[at]
    for copy in ring + w_z + w_y + w_all + near_core + near_x + far_core + far_x + y_copies + grad_core + grad_y + grad_z + grad_x + spread:
        copy.wait_send()


def per_device(features, sampled_slots, block_index, counts, weight, cotangent):
    hbm = pl.BlockSpec(memory_space=pl.ANY)
    vmem = pl.BlockSpec(memory_space=pltpu.VMEM)
    dma = pltpu.SemaphoreType.DMA
    return pl.pallas_call(
        layer_kernel,
        in_specs=[hbm, hbm, hbm, pl.BlockSpec(memory_space=pltpu.SMEM), hbm, hbm],
        out_specs=(vmem, vmem),
        scratch_shapes=[
            pltpu.VMEM((48, 16384), BF),
            pltpu.VMEM((128, 144, 128), BF),
            pltpu.VMEM((128, 48, 128), BF),
            pltpu.VMEM((8, 16, 1024), jnp.int32),
            pltpu.VMEM((8, 8, 1024), jnp.int32),
            pltpu.VMEM((128, 128), jnp.int32),
            pltpu.VMEM((128, 128), jnp.int32),
            pltpu.VMEM((64, 8, 128, 256), BF),
            pltpu.VMEM((4, 144, 1024), F32),
            pltpu.VMEM((4, 144, 1024), F32),
            pltpu.VMEM((4, 48, 1024), F32),
            pltpu.VMEM((4, 48, 1024), F32),
            pltpu.VMEM((3, 144, 1024), BF),
            pltpu.VMEM((3, 144, 1024), BF),
            pltpu.VMEM((3, 48, 1024), BF),
            pltpu.VMEM((3, 48, 1024), BF),
            pltpu.VMEM((144, 1024), F32),
            pltpu.VMEM((48, 1024), F32),
            pltpu.VMEM((8, 768, 128), BF),
            pltpu.VMEM((4, 192, 256), BF),
            pltpu.VMEM((4, 192, 256), BF),
            pltpu.VMEM((256, 768), BF),
            pltpu.VMEM((256, 1024), BF),
            pltpu.VMEM((2, 768, 256), F32),
            pltpu.VMEM((2, 768, 256), F32),
            pltpu.VMEM((6, 192, 256), BF),
            pltpu.VMEM((6, 192, 256), BF),
            pltpu.VMEM((2, 192, 256), F32),
            pltpu.VMEM((6, 48, 256), BF),
            pltpu.VMEM((6, 48, 256), BF),
            pltpu.VMEM((4, 48, 128), F32),
            pltpu.VMEM((3, 48, 128), F32),
            pltpu.VMEM((8, 48, 128), F32),
            dma((5,)), dma((2, 6)), dma((2, 13)), dma((2, 8)), dma((2, 6)), dma((2, 3)),
            dma((2, 2)), dma((2, 6)), dma((2, 6)), dma((2, 3)), dma((2, 7)),
        ],
        out_shape=(
            jax.ShapeDtypeStruct((256, 1024), BF),
            jax.ShapeDtypeStruct((48, 1024), F32),
        ),
        compiler_params=pltpu.CompilerParams(vmem_limit_bytes=63 << 20, collective_id=0, has_side_effects=True),
    )(features, sampled_slots, counts, block_index.reshape(8, 512), weight, cotangent)


def solution(mesh):
    placed = (
        P("feat", "batch"),
        P(None, "batch", None, None),
        P(None, "batch", None, None),
        P(),
        P("feat", None),
        P(("feat", "batch"), None),
    )
    return jax.shard_map(
        per_device,
        mesh=mesh,
        in_specs=placed,
        out_specs=(P(("feat", "batch"), None), P("feat", None)),
        check_vma=False,
    )
```

time: 185 us -> 118 us (0.64)
  waiting for transfers between devices: 64.3 us -> 0 us
  Pallas kernels: 89.3 us -> 112 us
  starting transfers between devices: 20.7 us -> 0 us
  matrix products: 6.69 us -> 0 us
  local copies, waits for them, and re-layouts: 1.74 us -> 5.13 us
    ppermute x15 -> x0, waiting for transfers between devices: 64.3 us -> none  [shift(): return lax.ppermute(array, axis, [(at, move(at)) for at in range(size)])]
    pallas_call x1, Pallas kernels: 89.3 us -> 112 us  [per_device(): pl.pallas_call(layer_kernel, in_specs=[hbm, hbm, hbm, pl.BlockSpec(memory...]
    ppermute x15 -> x0, starting transfers between devices: 20.7 us -> none  [shift(): return lax.ppermute(array, axis, [(at, move(at)) for at in range(size)])]
    dot_general x8 -> x0, matrix products: 6.69 us -> none  [the longest x4 5.6 us: per_device(): jnp.einsum('dr,dh->rh', block, weights, preferred_element_type=F32)]
    unnamed x10 -> x3, local copies, waits for them, and re-layouts: 0.97 us -> 4.41 us
  transfers between devices with their start and end apart: 15 -> 0, of which waited for: 11 -> 0; matrix products, arithmetic and copies ran while one was open for 2% -> 0% of each run, Pallas kernels for 48% -> 0%
where the time goes in v3:
time: 118 us
  Pallas kernels  112 us (95%)
  local copies, waits for them, and re-layouts  5.13 us (4%)
    pallas_call x1, Pallas kernels, per_device(): pl.pallas_call(layer_kernel, in_specs=[hbm, hbm, hbm, pl.BlockSpec(memory...  112 us
    unnamed x3, local copies, waits for them, and re-layouts  4.41 us

profile of v3, /device:TPU:1, one launch (start us, length us, event | category | flops | bytes accessed | tf_op | source)
XLA Modules:
  0.0 117.6 jit_solution(15134063720771233106)
XLA Ops:
  0.6 0.9 copy.9
  1.6 0.7 reshape.7.tiles
  2.3 111.8 %shard_map.77 = (bf16[256,1024]{1,0:T(8,128)(2,1)}, f32[48,1024]{1,0:T(8,128)}) custom-call(bf16[48,16384]{1,0:T(8,128)(2,1)} %features.1, s32[8,1,16,4096]{3,2,1,0:T(8,128)} %slots.1, s32[8,8,4096]{2,1,0:T(8,128)} %counts.1, s32[8,512]{1,0:T(8,128)} %reshape.7.tiles, bf16[48,1024]{1,0:T(8,128)(2,1)} %weight.1, bf16[256,1024]{1,0:T(8,128)(2,1)} %cotangent.1), custom_call_target="tpu_custom_call" | custom-call | tf_op jit(solution)/shard_map/pallas_call | solution.py:334
  114.1 1.9 %copy.12 = bf16[256,1024]{1,0:T(8,128)(2,1)} copy(bf16[256,1024]{1,0:T(8,128)(2,1)} %get-tuple-element.4) | data formatting | bytes 1048576
  116.0 1.6 %copy.13 = f32[48,1024]{1,0:T(8,128)} copy(f32[48,1024]{1,0:T(8,128)} %get-tuple-element.5) | data formatting | bytes 393216

commit v4 on v3

v4 whole, which is shorter than its diff:
```python
import jax
import jax.numpy as jnp
from jax import lax
from jax.experimental import pallas as pl
from jax.experimental.pallas import tpu as pltpu
from jax.sharding import PartitionSpec as P

BF = jnp.bfloat16
F32 = jnp.float32
NT = (((1,), (1,)), ((), ()))


def edge_codes(slots, used):
    slot_row = lax.broadcasted_iota(jnp.int32, slots.shape, 0) & 15
    lane = lax.broadcasted_iota(jnp.int32, slots.shape, 1)
    height = slots.shape[0]
    value = jnp.where(slot_row < used, slots, -1)
    for bit in range(4):
        rows, lanes = 1 << bit, 8 << bit
        row_bit = (slot_row >> bit) & 1
        lane_bit = (lane >> (bit + 3)) & 1
        later = pltpu.roll(pltpu.roll(value, height - rows, 0), lanes, 1)
        earlier = pltpu.roll(pltpu.roll(value, rows, 0), 128 - lanes, 1)
        value = jnp.where(row_bit < lane_bit, later, jnp.where(row_bit > lane_bit, earlier, value))
    return (value >> 7) * 8 + (lane & 7), value & 127


def onehot(code):
    rows = lax.broadcasted_iota(jnp.int32, (128, 128), 0).astype(BF)
    match = jnp.broadcast_to(code.astype(BF), (128, 128)) == rows
    return jnp.where(match, BF(1), BF(0))


def build(adjacency, pairs_at, block, tile_codes, node_codes):
    blank = jnp.zeros((128, 128), BF)

    def diagonal(first, second):
        return jnp.concatenate([jnp.concatenate([first, blank], 1), jnp.concatenate([blank, second], 1)], 0)

    for pair in range(8):
        row = block * 16 + 2 * pair
        tile_a, tile_b = onehot(tile_codes[pl.ds(row, 1)]), onehot(tile_codes[pl.ds(row + 1, 1)])
        node_a, node_b = onehot(node_codes[pl.ds(row, 1)]), onehot(node_codes[pl.ds(row + 1, 1)])
        if pair % 2 == 0:
            left, right = jnp.concatenate([tile_a, tile_b], 1), diagonal(node_a, node_b)
        else:
            left, right = diagonal(tile_a, tile_b), jnp.concatenate([node_a, node_b], 1)
        both = lax.dot_general(left, right, NT, preferred_element_type=F32)
        both_a, both_b = (both[:, :128], both[:, 128:]) if pair % 2 == 0 else (both[:128], both[128:])
        rows = jnp.concatenate([both_a.reshape(16, 8, 128), both_b.reshape(16, 8, 128)], 1).astype(BF)
        for tile in range(16):
            adjacency[pairs_at, tile // 2, pair * 16:pair * 16 + 16, tile % 2 * 128:tile % 2 * 128 + 128] = rows[tile]


def remote(src, dst, sems, at, target):
    return pltpu.make_async_remote_copy(
        src_ref=src, dst_ref=dst, send_sem=sems.at[0, at], recv_sem=sems.at[1, at],
        device_id=target, device_id_type=pl.DeviceIdType.MESH,
    )


TURN = (0, 1, 3, 2)


def layer_kernel(
    features, slots, counts, tiles, weight, cotangent, hidden, weight_grad,
    raw, feats, slot_rows, used, own_used, tile_codes, node_codes, adjacency,
    sums_out, sums_in, x_out, x_in, weights, rows, rows_t, cot,
    grad_out, grad_in, grad_y_out, grad_y_in, grad_own, grad_z_out, grad_z_in, grad_x_out, grad_x_in, pieces,
    load_sems, ring_sems, w_sems, sum_sems, x_sems, grad_core_sems, grad_y_sems, grad_z_sems, grad_x_sems, piece_sems,
):
    feat, batch = lax.axis_index("feat"), lax.axis_index("batch")
    z, y, x, core = feat // 4, feat % 4, batch // 2, batch % 2
    piece = core * 4 + x
    ring_at_me, cross_at_me = z + core * (y - z), y + core * (z - y)

    def feat_at(ring_place, cross_place):
        return ring_place * (4 - 3 * core) + cross_place * (1 + 3 * core)

    def batch_at(step, side):
        return lax.rem(x + step, 4) * 2 + lax.rem(core + side, 2)

    def ring_dev(step, side=0):
        return (feat_at(lax.rem(ring_at_me + step, 4), cross_at_me), batch_at(0, side))

    def cross_dev(step, side=0):
        return (feat_at(ring_at_me, lax.rem(cross_at_me + step, 4)), batch_at(0, side))

    def x_at(step, side=0):
        return (feat, batch_at(step, side))

    partner = x_at(0, 1)
    others = [x_at(step, side) for step in range(4) for side in range(2)][1:]
    barrier = pltpu.get_barrier_semaphore()
    greeted = [dev(step, side) for dev in (ring_dev, cross_dev) for side in range(2) for step in (1, 2, 3)] + others
    for device in greeted:
        pl.semaphore_signal(barrier, inc=1, device_id=device, device_id_type=pl.DeviceIdType.MESH)

    def owned(owner):
        return pl.ds(pl.multiple_of(owner * 256, 256), 256)

    piece_columns = pl.ds(pl.multiple_of(piece * 128, 128), 128)
    loads = [
        pltpu.make_async_copy(features, raw, load_sems.at[0]),
        pltpu.make_async_copy(weight.at[:, piece_columns], weights.at[piece, pl.ds(0, 48)], load_sems.at[1]),
        pltpu.make_async_copy(cotangent, cot, load_sems.at[2]),
        pltpu.make_async_copy(counts.at[batch, :, owned(feat)], own_used, load_sems.at[3]),
    ]
    for at in range(4):
        source, target = owned(feat_at(ring_at_me, at)), pl.ds(at * 256, 256)
        loads.append(pltpu.make_async_copy(slots.at[:, 0, :, source], slot_rows.at[:, :, target], load_sems.at[4 + 2 * at]))
        loads.append(pltpu.make_async_copy(counts.at[:, :, source], used.at[:, :, target], load_sems.at[5 + 2 * at]))
    for load in loads:
        load.start()
    loads[0].wait()
    for tile in range(128):
        feats[tile, 0:48, :] = raw[:, tile * 128:tile * 128 + 128]
    loads[1].wait()
    pl.semaphore_wait(barrier, len(greeted))

    low, high = pl.ds(0, 64), pl.ds(64, 64)

    def shard(at, part):
        return feats.at[part, pl.ds(48 * at, 48), :]

    ring = [
        remote(shard(0, low), shard(2, low), ring_sems, 0, ring_dev(1)),
        remote(shard(0, high), shard(1, high), ring_sems, 1, ring_dev(3)),
        remote(shard(0, high), shard(2, high), ring_sems, 2, ring_dev(1)),
        remote(shard(0, low), shard(1, low), ring_sems, 3, ring_dev(3)),
        remote(shard(2, low), shard(3, low), ring_sems, 4, ring_dev(1)),
        remote(shard(1, high), shard(3, high), ring_sems, 5, ring_dev(3)),
    ]

    mine = weights.at[piece]
    w_first = mine.at[pl.ds(0, 48)]
    w_z = [
        remote(w_first, mine.at[pl.ds(48 * {1: 2, 2: 3, 3: 1}[step], 48)], w_sems, step - 1, ring_dev(step))
        for step in (1, 2, 3)
    ]
    w_y = [
        remote(mine.at[pl.ds(0, 192)], mine.at[pl.ds(192 * (4 - step), 192)], w_sems, 2 + step, cross_dev(step))
        for step in (1, 2, 3)
    ]
    w_all = [
        remote(mine, mine, w_sems, 6 + at, device) for at, device in enumerate(others)
    ]
    for copy in w_z:
        copy.start()
    ring[0].start()
    ring[1].start()
    for load in loads[4:]:
        load.wait()

    def group_at(step):
        turn = step // 2
        away = turn + 2 - (turn // 2) * (2 * turn - 1)
        return batch_at(away, 1 - step % 2)

    def build_group(step, unused):
        group = group_at(step)
        group_used = used[group, pl.ds(batch, 1), :]
        tile_code, node_code = edge_codes(
            jnp.concatenate([slot_rows[group, :, b * 128:b * 128 + 128] for b in range(8)], 0),
            jnp.concatenate([jnp.broadcast_to(group_used[:, b * 128:b * 128 + 128], (16, 128)) for b in range(8)], 0),
        )
        tile_codes[...] = tile_code
        node_codes[...] = node_code

        def some(turn, unused):
            for at in range(4):
                build(adjacency, step * 8 + turn * 4 + at, turn * 4 + at, tile_codes, node_codes)
            return 0

        return lax.fori_loop(0, 2, some, 0)

    lax.fori_loop(0, 2, build_group, 0)
    ring[2].start()
    ring[3].start()
    for copy in w_z:
        copy.wait_recv()
    for copy in w_y:
        copy.start()
    lax.fori_loop(2, 5, build_group, 0)
    ring[0].wait_recv()
    ring[1].wait_recv()
    ring[4].start()
    ring[5].start()
    for copy in w_y:
        copy.wait_recv()
    for copy in w_all:
        copy.start()
    lax.fori_loop(5, 8, build_group, 0)
    for at in (2, 3, 4, 5):
        ring[at].wait_recv()

    def products(step):
        group = group_at(step)

        def some(turn, unused):
            for at in range(4):
                owner = turn * 2 + at // 2
                block = feat_at(ring_at_me, owner) * 2 + at % 2
                total = jnp.zeros((192, 128), F32)
                for pair in range(8):
                    halves = [feats[tiles[group, block * 16 + pair * 2 + half]] for half in range(2)]
                    total += lax.dot_general(
                        jnp.concatenate(halves, 1),
                        adjacency[step * 8 + turn * 4 + at, pair],
                        NT,
                        preferred_element_type=F32,
                    )
                sums_out[step * 4 + owner, :, at % 2 * 128:at % 2 * 128 + 128] = total.astype(BF)
            return 0

        lax.fori_loop(0, 2, some, 0)

    def sum_copies(turn, side):
        copies = []
        for step in range(1 - side, 4):
            copies.append(
                remote(
                    sums_out.at[(turn * 2 + 1 - side) * 4 + lax.rem(cross_at_me + step, 4)],
                    sums_in.at[turn * 8 + side * 4 + (4 - step) % 4],
                    sum_sems, turn * 7 + side * 3 + step - 1 + side, cross_dev(step, side),
                )
            )
        return copies

    def owner_sum(turn, across):
        first = sums_out[(turn * 2 + 1) * 4 + cross_at_me] if across == 0 else sums_in[turn * 8 + across]
        second = [
            sums_in[turn * 8 + 4 + TURN[slot], TURN[across] * 48:TURN[across] * 48 + 48, :] for slot in range(4)
        ]
        return first.astype(F32) + jnp.concatenate(second, 0).astype(F32)

    x_steps = (2, 3, 1)
    x_copies = [remote(x_out.at[turn], x_in.at[turn], x_sems, turn, x_at(x_steps[turn])) for turn in range(3)]
    all_sums = []

    def finish(turn):
        for copy in all_sums[turn]:
            copy.wait_recv()
        if turn < 3:
            for across in range(4):
                x_out[turn, across * 192:across * 192 + 192, :] = owner_sum(turn, across).astype(BF)
            x_copies[turn].start()

    for turn in range(4):
        copies = []
        for side in (1, 0):
            products(turn * 2 + 1 - side)
            new = sum_copies(turn, side)
            for copy in new:
                copy.start()
            copies += new
            if side == 1 and turn > 0:
                finish(turn - 1)
        all_sums.append(copies)
    loads[2].wait()
    loads[3].wait()
    for copy in w_all:
        copy.wait_recv()
    totals = jnp.sum(own_used[...], axis=0, keepdims=True).astype(F32)
    finish(3)
    for copy in x_copies:
        copy.wait_recv()
    for across in range(4):
        part = slice(across * 192, across * 192 + 192)
        summed = owner_sum(3, across)
        for turn in range(3):
            summed = summed + x_in[turn, part, :].astype(F32)
        rows[part, :] = (summed / totals).astype(BF)
    rows_t[...] = rows[...].T

    def swapped(part):
        return jnp.concatenate(
            [part[TURN[slot] * 192 + TURN[across] * 48:TURN[slot] * 192 + TURN[across] * 48 + 48]
             for across in range(4) for slot in range(4)],
            0,
        )

    def layer(tile, partners):
        columns = pl.ds(pl.multiple_of(tile * 256, 256), 256)
        part = jnp.concatenate([weights[tile * 2], weights[tile * 2 + 1]], 1)
        preact = jnp.dot(rows_t[...], swapped(part) if partners else part, preferred_element_type=F32)
        sigmoid_val = jax.nn.sigmoid(preact)
        hidden[:, columns] = (preact * sigmoid_val).astype(BF)
        pre_grad = cot[:, columns].astype(F32) * sigmoid_val * (1.0 + preact * (1.0 - sigmoid_val))
        return jnp.dot(rows[...], pre_grad.astype(BF), preferred_element_type=F32)

    grad_core = [remote(grad_out.at[at], grad_in.at[at], grad_core_sems, at, partner) for at in range(2)]
    for at in range(2):
        grad_out[at] = layer((1 - core) * 2 + at, True)
        grad_core[at].start()
    grad_y = []
    for at in range(2):
        grad = layer(core * 2 + at, False)
        grad_core[at].wait_recv()
        grad = grad + swapped(grad_in[at])
        grad_own[at] = grad[0:192]
        for step in (1, 2, 3):
            slot = at * 3 + step - 1
            grad_y_out[slot] = grad[step * 192:step * 192 + 192].astype(BF)
            grad_y.append(remote(grad_y_out.at[slot], grad_y_in.at[slot], grad_y_sems, slot, cross_dev(step)))
            grad_y[slot].start()
    grad_z = []
    for at in range(2):
        grad = grad_own[at]
        for step in (1, 2, 3):
            grad_y[at * 3 + step - 1].wait_recv()
            grad = grad + grad_y_in[at * 3 + step - 1].astype(F32)
        grad_own[at] = grad
        for shard_at, step in ((1, 1), (2, 3), (3, 2)):
            slot = at * 3 + shard_at - 1
            grad_z_out[slot] = grad[shard_at * 48:shard_at * 48 + 48].astype(BF)
            grad_z.append(remote(grad_z_out.at[slot], grad_z_in.at[slot], grad_z_sems, slot, ring_dev(step)))
            grad_z[slot].start()
    for at in range(2):
        grad = grad_own[at, 0:48]
        for slot in range(at * 3, at * 3 + 3):
            grad_z[slot].wait_recv()
            grad = grad + grad_z_in[slot].astype(F32)
        grad_x_out[at * 2] = grad[:, :128]
        grad_x_out[at * 2 + 1] = grad[:, 128:]
    grad_x = [
        remote(grad_x_out.at[lax.rem(x + step, 4)], grad_x_in.at[step - 1], grad_x_sems, step - 1, x_at(step))
        for step in (1, 2, 3)
    ]
    for copy in grad_x:
        copy.start()
    grad = grad_x_out[x]
    for step in range(3):
        grad_x[step].wait_recv()
        grad = grad + grad_x_in[step]
    pieces[piece] = grad
    spread = [remote(pieces.at[piece], pieces.at[piece], piece_sems, at, device) for at, device in enumerate(others)]
    for copy in spread:
        copy.start()
    for copy in spread:
        copy.wait_recv()
    for at in range(8):
        weight_grad[:, at * 128:at * 128 + 128] = pieces[at]
    for copy in ring + w_z + w_y + w_all + sum(all_sums, []) + x_copies + grad_core + grad_y + grad_z + grad_x + spread:
        copy.wait_send()


def per_device(features, sampled_slots, block_index, counts, weight, cotangent):
    hbm = pl.BlockSpec(memory_space=pl.ANY)
    vmem = pl.BlockSpec(memory_space=pltpu.VMEM)
    dma = pltpu.SemaphoreType.DMA
    return pl.pallas_call(
        layer_kernel,
        in_specs=[hbm, hbm, hbm, pl.BlockSpec(memory_space=pltpu.SMEM), hbm, hbm],
        out_specs=(vmem, vmem),
        scratch_shapes=[
            pltpu.VMEM((48, 16384), BF),
            pltpu.VMEM((128, 192, 128), BF),
            pltpu.VMEM((8, 16, 1024), jnp.int32),
            pltpu.VMEM((8, 8, 1024), jnp.int32),
            pltpu.VMEM((8, 256), jnp.int32),
            pltpu.VMEM((128, 128), jnp.int32),
            pltpu.VMEM((128, 128), jnp.int32),
            pltpu.VMEM((64, 8, 128, 256), BF),
            pltpu.VMEM((32, 192, 256), BF),
            pltpu.VMEM((32, 192, 256), BF),
            pltpu.VMEM((3, 768, 256), BF),
            pltpu.VMEM((3, 768, 256), BF),
            pltpu.VMEM((8, 768, 128), BF),
            pltpu.VMEM((768, 256), BF),
            pltpu.VMEM((256, 768), BF),
            pltpu.VMEM((256, 1024), BF),
            pltpu.VMEM((2, 768, 256), F32),
            pltpu.VMEM((2, 768, 256), F32),
            pltpu.VMEM((6, 192, 256), BF),
            pltpu.VMEM((6, 192, 256), BF),
            pltpu.VMEM((2, 192, 256), F32),
            pltpu.VMEM((6, 48, 256), BF),
            pltpu.VMEM((6, 48, 256), BF),
            pltpu.VMEM((4, 48, 128), F32),
            pltpu.VMEM((3, 48, 128), F32),
            pltpu.VMEM((8, 48, 128), F32),
            dma((12,)), dma((2, 6)), dma((2, 13)), dma((2, 28)), dma((2, 3)),
            dma((2, 2)), dma((2, 6)), dma((2, 6)), dma((2, 3)), dma((2, 7)),
        ],
        out_shape=(
            jax.ShapeDtypeStruct((256, 1024), BF),
            jax.ShapeDtypeStruct((48, 1024), F32),
        ),
        compiler_params=pltpu.CompilerParams(vmem_limit_bytes=63 << 20, collective_id=0, has_side_effects=True),
    )(features, sampled_slots, counts, block_index.reshape(8, 512), weight, cotangent)


def solution(mesh):
    placed = (
        P("feat", "batch"),
        P(None, "batch", None, None),
        P(None, "batch", None, None),
        P(),
        P("feat", None),
        P(("feat", "batch"), None),
    )
    return jax.shard_map(
        per_device,
        mesh=mesh,
        in_specs=placed,
        out_specs=(P(("feat", "batch"), None), P("feat", None)),
        check_vma=False,
    )
```

time: 118 us -> 101 us (0.86)
  Pallas kernels: 112 us -> 95.3 us
    pallas_call x1, Pallas kernels: 112 us -> 95.3 us  [per_device(): pl.pallas_call(layer_kernel, in_specs=[hbm, hbm, hbm, pl.BlockSpec(memory...]
where the time goes in v4:
time: 101 us
  Pallas kernels  95.3 us (94%)
  local copies, waits for them, and re-layouts  5.13 us (5%)
    pallas_call x1, Pallas kernels, per_device(): pl.pallas_call(layer_kernel, in_specs=[hbm, hbm, hbm, pl.BlockSpec(memory...  95.3 us
    unnamed x3, local copies, waits for them, and re-layouts  4.41 us

profile of v4, /device:TPU:1, one launch (start us, length us, event | category | flops | bytes accessed | tf_op | source)
XLA Modules:
  0.0 101.1 jit_solution(18212961860812155759)
XLA Ops:
  0.6 0.9 copy.9
  1.6 0.7 reshape.7.tiles
  2.3 95.3 %shard_map.77 = (bf16[256,1024]{1,0:T(8,128)(2,1)}, f32[48,1024]{1,0:T(8,128)}) custom-call(bf16[48,16384]{1,0:T(8,128)(2,1)} %features.1, s32[8,1,16,4096]{3,2,1,0:T(8,128)} %slots.1, s32[8,8,4096]{2,1,0:T(8,128)} %counts.1, s32[8,512]{1,0:T(8,128)} %reshape.7.tiles, bf16[48,1024]{1,0:T(8,128)(2,1)} %weight.1, bf16[256,1024]{1,0:T(8,128)(2,1)} %cotangent.1), custom_call_target="tpu_custom_call" | custom-call | tf_op jit(solution)/shard_map/pallas_call | solution.py:352
  97.6 1.9 %copy.12 = bf16[256,1024]{1,0:T(8,128)(2,1)} copy(bf16[256,1024]{1,0:T(8,128)(2,1)} %get-tuple-element.4) | data formatting | bytes 1048576
  99.5 1.6 %copy.13 = f32[48,1024]{1,0:T(8,128)} copy(f32[48,1024]{1,0:T(8,128)} %get-tuple-element.5) | data formatting | bytes 393216

commit v5 on v4

--- a/solution.py
+++ b/solution.py
@@ -63,11 +63,11 @@
 
 
 def layer_kernel(
-    features, slots, counts, tiles, weight, cotangent, hidden, weight_grad,
-    raw, feats, slot_rows, used, own_used, tile_codes, node_codes, adjacency,
-    sums_out, sums_in, x_out, x_in, weights, rows, rows_t, cot,
-    grad_out, grad_in, grad_y_out, grad_y_in, grad_own, grad_z_out, grad_z_in, grad_x_out, grad_x_in, pieces,
-    load_sems, ring_sems, w_sems, sum_sems, x_sems, grad_core_sems, grad_y_sems, grad_z_sems, grad_x_sems, piece_sems,
+    features, slots, counts, block_index, weight, cotangent, hidden, weight_grad,
+    tiles, raw, feats, slot_rows, used, own_used, tile_codes, node_codes, adjacency,
+    sums_out, sums_in, x_out, x_in, relay_in, weights, rows, rows_t, cot,
+    grad_out, grad_in, grad_y_out, grad_y_in, grad_own, grad_own_slice, grad_z_out, grad_z_in, pieces,
+    load_sems, ring_sems, w_sems, sum_sems, x_sems, grad_core_sems, grad_y_sems, grad_z_sems, piece_sems,
 ):
     feat, batch = lax.axis_index("feat"), lax.axis_index("batch")
     z, y, x, core = feat // 4, feat % 4, batch // 2, batch % 2
@@ -93,6 +93,9 @@
     others = [x_at(step, side) for step in range(4) for side in range(2)][1:]
     barrier = pltpu.get_barrier_semaphore()
     greeted = [dev(step, side) for dev in (ring_dev, cross_dev) for side in range(2) for step in (1, 2, 3)] + others
+    greeted += [
+        (feat_at(lax.rem(ring_at_me + step, 4), cross_at_me), batch_at(x_step, 0)) for step in (1, 2, 3) for x_step in (1, 2, 3)
+    ]
     for device in greeted:
         pl.semaphore_signal(barrier, inc=1, device_id=device, device_id_type=pl.DeviceIdType.MESH)
 
@@ -105,6 +108,7 @@
         pltpu.make_async_copy(weight.at[:, piece_columns], weights.at[piece, pl.ds(0, 48)], load_sems.at[1]),
         pltpu.make_async_copy(cotangent, cot, load_sems.at[2]),
         pltpu.make_async_copy(counts.at[batch, :, owned(feat)], own_used, load_sems.at[3]),
+        pltpu.make_async_copy(block_index.at[:, 0], tiles, load_sems.at[12]),
     ]
     for at in range(4):
         source, target = owned(feat_at(ring_at_me, at)), pl.ds(at * 256, 256)
@@ -203,7 +207,7 @@
                 block = feat_at(ring_at_me, owner) * 2 + at % 2
                 total = jnp.zeros((192, 128), F32)
                 for pair in range(8):
-                    halves = [feats[tiles[group, block * 16 + pair * 2 + half]] for half in range(2)]
+                    halves = [feats[tiles[group, pair * 2 + half, block]] for half in range(2)]
                     total += lax.dot_general(
                         jnp.concatenate(halves, 1),
                         adjacency[step * 8 + turn * 4 + at, pair],
@@ -234,17 +238,26 @@
         ]
         return first.astype(F32) + jnp.concatenate(second, 0).astype(F32)
 
-    x_steps = (2, 3, 1)
-    x_copies = [remote(x_out.at[turn], x_in.at[turn], x_sems, turn, x_at(x_steps[turn])) for turn in range(3)]
+    relays = [
+        remote(x_out.at[0, pl.ds(384 * at, 384)], relay_in.at[at], x_sems, at, x_at(1 + 2 * at)) for at in range(2)
+    ]
+    x_copies = [remote(x_out.at[1 + at], x_in.at[at], x_sems, 2 + at, x_at(3 - 2 * at)) for at in range(2)]
     all_sums = []
 
     def finish(turn):
         for copy in all_sums[turn]:
             copy.wait_recv()
-        if turn < 3:
-            for across in range(4):
-                x_out[turn, across * 192:across * 192 + 192, :] = owner_sum(turn, across).astype(BF)
-            x_copies[turn].start()
+        if turn == 3:
+            return
+        if turn > 0:
+            relays[2 - turn].wait_recv()
+        for across in range(4):
+            total = owner_sum(turn, across)
+            if turn > 0 and across // 2 == 2 - turn:
+                total = total + relay_in[across // 2, across % 2 * 192:across % 2 * 192 + 192, :].astype(F32)
+            x_out[turn, across * 192:across * 192 + 192, :] = total.astype(BF)
+        for copy in relays if turn == 0 else [x_copies[turn - 1]]:
+            copy.start()
 
     for turn in range(4):
         copies = []
@@ -268,7 +281,7 @@
     for across in range(4):
         part = slice(across * 192, across * 192 + 192)
         summed = owner_sum(3, across)
-        for turn in range(3):
+        for turn in range(2):
             summed = summed + x_in[turn, part, :].astype(F32)
         rows[part, :] = (summed / totals).astype(BF)
     rows_t[...] = rows[...].T
@@ -304,35 +317,29 @@
             grad_y_out[slot] = grad[step * 192:step * 192 + 192].astype(BF)
             grad_y.append(remote(grad_y_out.at[slot], grad_y_in.at[slot], grad_y_sems, slot, cross_dev(step)))
             grad_y[slot].start()
-    grad_z = []
     for at in range(2):
         grad = grad_own[at]
         for step in (1, 2, 3):
             grad_y[at * 3 + step - 1].wait_recv()
             grad = grad + grad_y_in[at * 3 + step - 1].astype(F32)
-        grad_own[at] = grad
-        for shard_at, step in ((1, 1), (2, 3), (3, 2)):
-            slot = at * 3 + shard_at - 1
-            grad_z_out[slot] = grad[shard_at * 48:shard_at * 48 + 48].astype(BF)
-            grad_z.append(remote(grad_z_out.at[slot], grad_z_in.at[slot], grad_z_sems, slot, ring_dev(step)))
-            grad_z[slot].start()
-    for at in range(2):
-        grad = grad_own[at, 0:48]
-        for slot in range(at * 3, at * 3 + 3):
-            grad_z[slot].wait_recv()
-            grad = grad + grad_z_in[slot].astype(F32)
-        grad_x_out[at * 2] = grad[:, :128]
-        grad_x_out[at * 2 + 1] = grad[:, 128:]
-    grad_x = [
-        remote(grad_x_out.at[lax.rem(x + step, 4)], grad_x_in.at[step - 1], grad_x_sems, step - 1, x_at(step))
-        for step in (1, 2, 3)
-    ]
-    for copy in grad_x:
-        copy.start()
-    grad = grad_x_out[x]
-    for step in range(3):
-        grad_x[step].wait_recv()
-        grad = grad + grad_x_in[step]
+        for half in range(2):
+            columns = slice(half * 128, half * 128 + 128)
+            grad_own_slice[at * 2 + half] = grad[0:48, columns]
+            for slot in range(4):
+                grad_z_out[(at * 2 + half) * 4 + slot] = grad[slot * 48:slot * 48 + 48, columns].astype(BF)
+    grad_z = [
+        remote(
+            grad_z_out.at[lax.rem(x + step, 4) * 4 + slot], grad_z_in.at[step * 4 + slot - 1], grad_z_sems, step * 4 + slot - 1,
+            (feat_at(lax.rem(ring_at_me + TURN[slot], 4), cross_at_me), batch_at(step, 0)),
+        )
+        for step in range(4) for slot in range(4) if step + slot > 0
+    ]
+    for copy in grad_z:
+        copy.start()
+    grad = grad_own_slice[x]
+    for at in range(15):
+        grad_z[at].wait_recv()
+        grad = grad + grad_z_in[at].astype(F32)
     pieces[piece] = grad
     spread = [remote(pieces.at[piece], pieces.at[piece], piece_sems, at, device) for at, device in enumerate(others)]
     for copy in spread:
@@ -341,19 +348,31 @@
         copy.wait_recv()
     for at in range(8):
         weight_grad[:, at * 128:at * 128 + 128] = pieces[at]
-    for copy in ring + w_z + w_y + w_all + sum(all_sums, []) + x_copies + grad_core + grad_y + grad_z + grad_x + spread:
+    for copy in ring + w_z + w_y + w_all + sum(all_sums, []) + relays + x_copies + grad_core + grad_y + grad_z + spread:
         copy.wait_send()
+
+
+def place_kernel(hidden, weight_grad, hidden_out, weight_grad_out, sems):
+    copies = [
+        pltpu.make_async_copy(hidden, hidden_out, sems.at[0]),
+        pltpu.make_async_copy(weight_grad, weight_grad_out, sems.at[1]),
+    ]
+    for copy in copies:
+        copy.start()
+    for copy in copies:
+        copy.wait()
 
 
 def per_device(features, sampled_slots, block_index, counts, weight, cotangent):
     hbm = pl.BlockSpec(memory_space=pl.ANY)
     vmem = pl.BlockSpec(memory_space=pltpu.VMEM)
     dma = pltpu.SemaphoreType.DMA
-    return pl.pallas_call(
+    outs = pl.pallas_call(
         layer_kernel,
-        in_specs=[hbm, hbm, hbm, pl.BlockSpec(memory_space=pltpu.SMEM), hbm, hbm],
+        in_specs=[hbm] * 6,
         out_specs=(vmem, vmem),
         scratch_shapes=[
+            pltpu.SMEM((8, 16, 32), jnp.int32),
             pltpu.VMEM((48, 16384), BF),
             pltpu.VMEM((128, 192, 128), BF),
             pltpu.VMEM((8, 16, 1024), jnp.int32),
@@ -365,7 +384,8 @@
             pltpu.VMEM((32, 192, 256), BF),
             pltpu.VMEM((32, 192, 256), BF),
             pltpu.VMEM((3, 768, 256), BF),
-            pltpu.VMEM((3, 768, 256), BF),
+            pltpu.VMEM((2, 768, 256), BF),
+            pltpu.VMEM((2, 384, 256), BF),
             pltpu.VMEM((8, 768, 128), BF),
             pltpu.VMEM((768, 256), BF),
             pltpu.VMEM((256, 768), BF),
@@ -375,20 +395,30 @@
             pltpu.VMEM((6, 192, 256), BF),
             pltpu.VMEM((6, 192, 256), BF),
             pltpu.VMEM((2, 192, 256), F32),
-            pltpu.VMEM((6, 48, 256), BF),
-            pltpu.VMEM((6, 48, 256), BF),
             pltpu.VMEM((4, 48, 128), F32),
-            pltpu.VMEM((3, 48, 128), F32),
+            pltpu.VMEM((16, 48, 128), BF),
+            pltpu.VMEM((15, 48, 128), BF),
             pltpu.VMEM((8, 48, 128), F32),
-            dma((12,)), dma((2, 6)), dma((2, 13)), dma((2, 28)), dma((2, 3)),
-            dma((2, 2)), dma((2, 6)), dma((2, 6)), dma((2, 3)), dma((2, 7)),
+            dma((13,)), dma((2, 6)), dma((2, 13)), dma((2, 28)), dma((2, 4)),
+            dma((2, 2)), dma((2, 6)), dma((2, 15)), dma((2, 7)),
         ],
         out_shape=(
             jax.ShapeDtypeStruct((256, 1024), BF),
             jax.ShapeDtypeStruct((48, 1024), F32),
         ),
         compiler_params=pltpu.CompilerParams(vmem_limit_bytes=63 << 20, collective_id=0, has_side_effects=True),
-    )(features, sampled_slots, counts, block_index.reshape(8, 512), weight, cotangent)
+    )(features, sampled_slots, counts, jnp.swapaxes(block_index, 2, 3), weight, cotangent)
+    return pl.pallas_call(
+        place_kernel,
+        in_specs=[hbm, hbm],
+        out_specs=(hbm, hbm),
+        scratch_shapes=[dma((2,))],
+        out_shape=(
+            jax.ShapeDtypeStruct((256, 1024), BF),
+            jax.ShapeDtypeStruct((48, 1024), F32),
+        ),
+        compiler_params=pltpu.CompilerParams(vmem_limit_bytes=63 << 20),
+    )(*outs)
 
 
 def solution(mesh):

time: 101 us -> 118 us (1.17)
  Pallas kernels: 95.3 us -> 117 us
  local copies, waits for them, and re-layouts: 5.13 us -> 0 us
    pallas_call x1 -> x2, Pallas kernels: 95.3 us -> 117 us  [the longest x1 93.9 us: per_device(): pl.pallas_call(layer_kernel, in_specs=[hbm] * 6, out_specs=(vmem, vmem),...]
    unnamed x3 -> x0, local copies, waits for them, and re-layouts: 4.41 us -> none
where the time goes in v5:
time: 118 us; the launch traced here: 117 us
  Pallas kernels  117 us (99%)
    pallas_call x1, Pallas kernels, per_device(): pl.pallas_call(layer_kernel, in_specs=[hbm] * 6, out_specs=(vmem, vmem),...  93.9 us
    pallas_call x1, Pallas kernels, per_device(): pl.pallas_call(place_kernel, in_specs=[hbm, hbm], out_specs=(hbm, hbm), s...  23 us

profile of v5, /device:TPU:1, one launch (start us, length us, event | category | flops | bytes accessed | tf_op | source)
XLA Modules:
  0.0 117.5 jit_solution(11662498649401470550)
XLA Ops:
  0.6 93.9 %shard_map.77 = (bf16[256,1024]{1,0:T(8,128)(2,1)}, f32[48,1024]{1,0:T(8,128)}) custom-call(bf16[48,16384]{1,0:T(8,128)(2,1)} %features.1, s32[8,1,16,4096]{3,2,1,0:T(8,128)} %slots.1, s32[8,8,4096]{2,1,0:T(8,128)} %counts.1, s32[8,1,16,32]{3,2,1,0:T(8,128)} %bitcast.1, bf16[48,1024]{1,0:T(8,128)(2,1)} %weight.1, bf16[256,1024]{1,0:T(8,128)(2,1)} %cotangent.1), custom_call_target="tpu_custom_call" | custom-call | tf_op jit(solution)/shard_map/pallas_call | solution.py:370
  94.5 23.0 %shard_map.78 = (bf16[256,1024]{1,0:T(8,128)(2,1)}, f32[48,1024]{1,0:T(8,128)}) custom-call(bf16[256,1024]{1,0:T(8,128)(2,1)} %get-tuple-element.4.hidden, f32[48,1024]{1,0:T(8,128)} %get-tuple-element.5.weight_grad), custom_call_target="tpu_custom_call" | custom-call | tf_op jit(solution)/shard_map/pallas_call | solution.py:411

commit v6 on v5

--- a/solution.py
+++ b/solution.py
@@ -352,22 +352,11 @@
         copy.wait_send()
 
 
-def place_kernel(hidden, weight_grad, hidden_out, weight_grad_out, sems):
-    copies = [
-        pltpu.make_async_copy(hidden, hidden_out, sems.at[0]),
-        pltpu.make_async_copy(weight_grad, weight_grad_out, sems.at[1]),
-    ]
-    for copy in copies:
-        copy.start()
-    for copy in copies:
-        copy.wait()
-
-
 def per_device(features, sampled_slots, block_index, counts, weight, cotangent):
     hbm = pl.BlockSpec(memory_space=pl.ANY)
     vmem = pl.BlockSpec(memory_space=pltpu.VMEM)
     dma = pltpu.SemaphoreType.DMA
-    outs = pl.pallas_call(
+    return pl.pallas_call(
         layer_kernel,
         in_specs=[hbm] * 6,
         out_specs=(vmem, vmem),
@@ -408,17 +397,6 @@
         ),
         compiler_params=pltpu.CompilerParams(vmem_limit_bytes=63 << 20, collective_id=0, has_side_effects=True),
     )(features, sampled_slots, counts, jnp.swapaxes(block_index, 2, 3), weight, cotangent)
-    return pl.pallas_call(
-        place_kernel,
-        in_specs=[hbm, hbm],
-        out_specs=(hbm, hbm),
-        scratch_shapes=[dma((2,))],
-        out_shape=(
-            jax.ShapeDtypeStruct((256, 1024), BF),
-            jax.ShapeDtypeStruct((48, 1024), F32),
-        ),
-        compiler_params=pltpu.CompilerParams(vmem_limit_bytes=63 << 20),
-    )(*outs)
 
 
 def solution(mesh):

time: 118 us -> 98.2 us (0.83)
  Pallas kernels: 117 us -> 93.9 us
  local copies, waits for them, and re-layouts: 0 us -> 3.48 us
    pallas_call x1 -> x0, Pallas kernels: 23 us -> none  [per_device(): pl.pallas_call(place_kernel, in_specs=[hbm, hbm], out_specs=(hbm, hbm), s...]
    unnamed x0 -> x2, local copies, waits for them, and re-layouts: none -> 3.48 us
where the time goes in v6:
time: 98.2 us; the launch traced here: 98 us
  Pallas kernels  93.9 us (96%)
  local copies, waits for them, and re-layouts  3.48 us (4%)
    pallas_call x1, Pallas kernels, per_device(): pl.pallas_call(layer_kernel, in_specs=[hbm] * 6, out_specs=(vmem, vmem),...  93.9 us
    unnamed x2, local copies, waits for them, and re-layouts  3.48 us

profile of v6, /device:TPU:1, one launch (start us, length us, event | category | flops | bytes accessed | tf_op | source)
XLA Modules:
  0.0 98.0 jit_solution(4222568419330081053)
XLA Ops:
  0.6 93.9 %shard_map.77 = (bf16[256,1024]{1,0:T(8,128)(2,1)}, f32[48,1024]{1,0:T(8,128)}) custom-call(bf16[48,16384]{1,0:T(8,128)(2,1)} %features.1, s32[8,1,16,4096]{3,2,1,0:T(8,128)} %slots.1, s32[8,8,4096]{2,1,0:T(8,128)} %counts.1, s32[8,1,16,32]{3,2,1,0:T(8,128)} %bitcast.1, bf16[48,1024]{1,0:T(8,128)(2,1)} %weight.1, bf16[256,1024]{1,0:T(8,128)(2,1)} %cotangent.1), custom_call_target="tpu_custom_call" | custom-call | tf_op jit(solution)/shard_map/pallas_call | solution.py:359
  94.5 1.9 %copy.10 = bf16[256,1024]{1,0:T(8,128)(2,1)} copy(bf16[256,1024]{1,0:T(8,128)(2,1)} %get-tuple-element.4) | data formatting | bytes 1048576
  96.4 1.6 %copy.11 = f32[48,1024]{1,0:T(8,128)} copy(f32[48,1024]{1,0:T(8,128)} %get-tuple-element.5) | data formatting | bytes 393216

commit v7 on v6

--- a/solution.py
+++ b/solution.py
@@ -158,8 +158,10 @@
 
     def group_at(step):
         turn = step // 2
-        away = turn + 2 - (turn // 2) * (2 * turn - 1)
-        return batch_at(away, 1 - step % 2)
+        side = 1 - step % 2
+        owner_core = core + side * (1 - 2 * core)
+        away = turn + 2 - (turn // 2) * (2 * turn - 1) + turn * (3 - turn) // 2 * (2 * turn - 3) * 2 * owner_core
+        return batch_at(away, side)
 
     def build_group(step, unused):
         group = group_at(step)
@@ -238,10 +240,11 @@
         ]
         return first.astype(F32) + jnp.concatenate(second, 0).astype(F32)
 
+    x_second, x_third = 3 - 2 * core, 1 + 2 * core
     relays = [
-        remote(x_out.at[0, pl.ds(384 * at, 384)], relay_in.at[at], x_sems, at, x_at(1 + 2 * at)) for at in range(2)
-    ]
-    x_copies = [remote(x_out.at[1 + at], x_in.at[at], x_sems, 2 + at, x_at(3 - 2 * at)) for at in range(2)]
+        remote(x_out.at[0, pl.ds(384 * at, 384)], relay_in.at[at], x_sems, at, x_at((x_third, x_second)[at])) for at in range(2)
+    ]
+    x_copies = [remote(x_out.at[1 + at], x_in.at[at], x_sems, 2 + at, x_at((x_second, x_third)[at])) for at in range(2)]
     all_sums = []
 
     def finish(turn):
@@ -302,31 +305,34 @@
         pre_grad = cot[:, columns].astype(F32) * sigmoid_val * (1.0 + preact * (1.0 - sigmoid_val))
         return jnp.dot(rows[...], pre_grad.astype(BF), preferred_element_type=F32)
 
-    grad_core = [remote(grad_out.at[at], grad_in.at[at], grad_core_sems, at, partner) for at in range(2)]
+    halves = (slice(0, 128), slice(128, 256))
+    grad_core = [remote(grad_out.at[at], grad_in.at[at], grad_core_sems, at, partner) for at in range(4)]
     for at in range(2):
-        grad_out[at] = layer((1 - core) * 2 + at, True)
-        grad_core[at].start()
+        grad = layer((1 - core) * 2 + at, True)
+        for half in range(2):
+            grad_out[at * 2 + half] = grad[:, halves[half]]
+            grad_core[at * 2 + half].start()
     grad_y = []
     for at in range(2):
-        grad = layer(core * 2 + at, False)
-        grad_core[at].wait_recv()
-        grad = grad + swapped(grad_in[at])
-        grad_own[at] = grad[0:192]
+        own_grad = layer(core * 2 + at, False)
+        for half in range(2):
+            part = at * 2 + half
+            grad_core[part].wait_recv()
+            grad = own_grad[:, halves[half]] + swapped(grad_in[part])
+            grad_own[part] = grad[0:192]
+            for step in (1, 2, 3):
+                slot = part * 3 + step - 1
+                grad_y_out[slot] = grad[step * 192:step * 192 + 192].astype(BF)
+                grad_y.append(remote(grad_y_out.at[slot], grad_y_in.at[slot], grad_y_sems, slot, cross_dev(step)))
+                grad_y[slot].start()
+    for part in range(4):
+        grad = grad_own[part]
         for step in (1, 2, 3):
-            slot = at * 3 + step - 1
-            grad_y_out[slot] = grad[step * 192:step * 192 + 192].astype(BF)
-            grad_y.append(remote(grad_y_out.at[slot], grad_y_in.at[slot], grad_y_sems, slot, cross_dev(step)))
-            grad_y[slot].start()
-    for at in range(2):
-        grad = grad_own[at]
-        for step in (1, 2, 3):
-            grad_y[at * 3 + step - 1].wait_recv()
-            grad = grad + grad_y_in[at * 3 + step - 1].astype(F32)
-        for half in range(2):
-            columns = slice(half * 128, half * 128 + 128)
-            grad_own_slice[at * 2 + half] = grad[0:48, columns]
-            for slot in range(4):
-                grad_z_out[(at * 2 + half) * 4 + slot] = grad[slot * 48:slot * 48 + 48, columns].astype(BF)
+            grad_y[part * 3 + step - 1].wait_recv()
+            grad = grad + grad_y_in[part * 3 + step - 1].astype(F32)
+        grad_own_slice[part] = grad[0:48]
+        for slot in range(4):
+            grad_z_out[part * 4 + slot] = grad[slot * 48:slot * 48 + 48].astype(BF)
     grad_z = [
         remote(
             grad_z_out.at[lax.rem(x + step, 4) * 4 + slot], grad_z_in.at[step * 4 + slot - 1], grad_z_sems, step * 4 + slot - 1,
@@ -379,17 +385,17 @@
             pltpu.VMEM((768, 256), BF),
             pltpu.VMEM((256, 768), BF),
             pltpu.VMEM((256, 1024), BF),
-            pltpu.VMEM((2, 768, 256), F32),
-            pltpu.VMEM((2, 768, 256), F32),
-            pltpu.VMEM((6, 192, 256), BF),
-            pltpu.VMEM((6, 192, 256), BF),
-            pltpu.VMEM((2, 192, 256), F32),
+            pltpu.VMEM((4, 768, 128), F32),
+            pltpu.VMEM((4, 768, 128), F32),
+            pltpu.VMEM((12, 192, 128), BF),
+            pltpu.VMEM((12, 192, 128), BF),
+            pltpu.VMEM((4, 192, 128), F32),
             pltpu.VMEM((4, 48, 128), F32),
             pltpu.VMEM((16, 48, 128), BF),
             pltpu.VMEM((15, 48, 128), BF),
             pltpu.VMEM((8, 48, 128), F32),
             dma((13,)), dma((2, 6)), dma((2, 13)), dma((2, 28)), dma((2, 4)),
-            dma((2, 2)), dma((2, 6)), dma((2, 15)), dma((2, 7)),
+            dma((2, 4)), dma((2, 12)), dma((2, 15)), dma((2, 7)),
         ],
         out_shape=(
             jax.ShapeDtypeStruct((256, 1024), BF),

time: 98.2 us -> 97.4 us (level)
  no operation moved by 1% of the time
where the time goes in v7:
time: 97.4 us; the launch traced here: 97.2 us
  Pallas kernels  93.1 us (96%)
  local copies, waits for them, and re-layouts  3.48 us (4%)
    pallas_call x1, Pallas kernels, per_device(): pl.pallas_call(layer_kernel, in_specs=[hbm] * 6, out_specs=(vmem, vmem),...  93.1 us
    unnamed x2, local copies, waits for them, and re-layouts  3.48 us

profile of v7, /device:TPU:1, one launch (start us, length us, event | category | flops | bytes accessed | tf_op | source)
XLA Modules:
  0.0 97.2 jit_solution(18357616558548312155)
XLA Ops:
  0.6 93.1 %shard_map.77 = (bf16[256,1024]{1,0:T(8,128)(2,1)}, f32[48,1024]{1,0:T(8,128)}) custom-call(bf16[48,16384]{1,0:T(8,128)(2,1)} %features.1, s32[8,1,16,4096]{3,2,1,0:T(8,128)} %slots.1, s32[8,8,4096]{2,1,0:T(8,128)} %counts.1, s32[8,1,16,32]{3,2,1,0:T(8,128)} %bitcast.1, bf16[48,1024]{1,0:T(8,128)(2,1)} %weight.1, bf16[256,1024]{1,0:T(8,128)(2,1)} %cotangent.1), custom_call_target="tpu_custom_call" | custom-call | tf_op jit(solution)/shard_map/pallas_call | solution.py:365
  93.8 1.9 %copy.10 = bf16[256,1024]{1,0:T(8,128)(2,1)} copy(bf16[256,1024]{1,0:T(8,128)(2,1)} %get-tuple-element.4) | data formatting | bytes 1048576
  95.6 1.6 %copy.11 = f32[48,1024]{1,0:T(8,128)} copy(f32[48,1024]{1,0:T(8,128)} %get-tuple-element.5) | data formatting | bytes 393216

commit v8 on v7

--- a/solution.py
+++ b/solution.py
@@ -264,13 +264,13 @@
 
     for turn in range(4):
         copies = []
-        for side in (1, 0):
+        for side in (0, 1):
             products(turn * 2 + 1 - side)
             new = sum_copies(turn, side)
             for copy in new:
                 copy.start()
             copies += new
-            if side == 1 and turn > 0:
+            if side == 0 and turn > 0:
                 finish(turn - 1)
         all_sums.append(copies)
     loads[2].wait()

time: 97.4 us -> 95.8 us (0.984)
  Pallas kernels: 93.1 us -> 91.4 us
    pallas_call x1, Pallas kernels: 93.1 us -> 91.4 us  [per_device(): pl.pallas_call(layer_kernel, in_specs=[hbm] * 6, out_specs=(vmem, vmem),...]
where the time goes in v8:
time: 95.8 us; the launch traced here: 95.6 us
  Pallas kernels  91.4 us (95%)
  local copies, waits for them, and re-layouts  3.48 us (4%)
    pallas_call x1, Pallas kernels, per_device(): pl.pallas_call(layer_kernel, in_specs=[hbm] * 6, out_specs=(vmem, vmem),...  91.4 us
    unnamed x2, local copies, waits for them, and re-layouts  3.48 us

profile of v8, /device:TPU:1, one launch (start us, length us, event | category | flops | bytes accessed | tf_op | source)
XLA Modules:
  0.0 95.6 jit_solution(12150170711621755951)
XLA Ops:
  0.6 91.4 %shard_map.77 = (bf16[256,1024]{1,0:T(8,128)(2,1)}, f32[48,1024]{1,0:T(8,128)}) custom-call(bf16[48,16384]{1,0:T(8,128)(2,1)} %features.1, s32[8,1,16,4096]{3,2,1,0:T(8,128)} %slots.1, s32[8,8,4096]{2,1,0:T(8,128)} %counts.1, s32[8,1,16,32]{3,2,1,0:T(8,128)} %bitcast.1, bf16[48,1024]{1,0:T(8,128)(2,1)} %weight.1, bf16[256,1024]{1,0:T(8,128)(2,1)} %cotangent.1), custom_call_target="tpu_custom_call" | custom-call | tf_op jit(solution)/shard_map/pallas_call | solution.py:365
  92.1 1.9 %copy.10 = bf16[256,1024]{1,0:T(8,128)(2,1)} copy(bf16[256,1024]{1,0:T(8,128)(2,1)} %get-tuple-element.4) | data formatting | bytes 1048576
  93.9 1.6 %copy.11 = f32[48,1024]{1,0:T(8,128)} copy(f32[48,1024]{1,0:T(8,128)} %get-tuple-element.5) | data formatting | bytes 393216

commit v9 on v8

--- a/solution.py
+++ b/solution.py
@@ -187,7 +187,7 @@
         copy.wait_recv()
     for copy in w_y:
         copy.start()
-    lax.fori_loop(2, 5, build_group, 0)
+    lax.fori_loop(2, 4, build_group, 0)
     ring[0].wait_recv()
     ring[1].wait_recv()
     ring[4].start()
@@ -196,7 +196,7 @@
         copy.wait_recv()
     for copy in w_all:
         copy.start()
-    lax.fori_loop(5, 8, build_group, 0)
+    lax.fori_loop(4, 8, build_group, 0)
     for at in (2, 3, 4, 5):
         ring[at].wait_recv()
 

time: 95.8 us -> 95.8 us (level)
  no operation moved by 1% of the time
where the time goes in v9:
time: 95.8 us; the launch traced here: 95.6 us
  Pallas kernels  91.4 us (95%)
  local copies, waits for them, and re-layouts  3.48 us (4%)
    pallas_call x1, Pallas kernels, per_device(): pl.pallas_call(layer_kernel, in_specs=[hbm] * 6, out_specs=(vmem, vmem),...  91.4 us
    unnamed x2, local copies, waits for them, and re-layouts  3.48 us

profile of v9, /device:TPU:1, one launch (start us, length us, event | category | flops | bytes accessed | tf_op | source)
XLA Modules:
  0.0 95.6 jit_solution(6863488295071365668)
XLA Ops:
  0.6 91.4 %shard_map.77 = (bf16[256,1024]{1,0:T(8,128)(2,1)}, f32[48,1024]{1,0:T(8,128)}) custom-call(bf16[48,16384]{1,0:T(8,128)(2,1)} %features.1, s32[8,1,16,4096]{3,2,1,0:T(8,128)} %slots.1, s32[8,8,4096]{2,1,0:T(8,128)} %counts.1, s32[8,1,16,32]{3,2,1,0:T(8,128)} %bitcast.1, bf16[48,1024]{1,0:T(8,128)(2,1)} %weight.1, bf16[256,1024]{1,0:T(8,128)(2,1)} %cotangent.1), custom_call_target="tpu_custom_call" | custom-call | tf_op jit(solution)/shard_map/pallas_call | solution.py:365
  92.1 1.9 %copy.10 = bf16[256,1024]{1,0:T(8,128)(2,1)} copy(bf16[256,1024]{1,0:T(8,128)(2,1)} %get-tuple-element.4) | data formatting | bytes 1048576
  93.9 1.6 %copy.11 = f32[48,1024]{1,0:T(8,128)} copy(f32[48,1024]{1,0:T(8,128)} %get-tuple-element.5) | data formatting | bytes 393216
